TPU v7x, 256 devices: a whole 4x4x8 slice. The times are simulated.
256 devices in a mesh: rows: 4 (over y), cols: 64 (over x, z, core).
Axes of the slice: x: 4, y: 4, z: 8, core: 2. Of those that a mesh axis runs over, the one named last changes fastest.
Arguments:
- sensitivity: bfloat16 [4, 256, 512, 512], P('rows', 'cols'), may hold values from -0.25 to 0.25
- tile_rows: int32 [4, 256], P('rows', 'cols'), may hold values from 0 to 127, as said below
- tile_cols: int32 [4, 256], P('rows', 'cols'), may hold values from 0 to 1, as said below
- kept_counts: int32 [4, 256], P('rows', 'cols'), may hold values from 0 to 512, as said below
- misfit: float32 [262144], P('rows'), may hold values from -6 to 6
- data_weight: float32 [262144], P('rows'), may hold values from 0.3 to 3
- depth_weight: float32 [65536], P('cols'), may hold values from 0.25 to 3
- density: float32 [65536], P('cols'), may hold values from -6 to 6
Outputs:
- new_density: float32 [65536], P('cols')
- new_misfit: float32 [262144], P(('rows', 'cols'))
Inputs may be any that keep to these rules, and one draw needn't show every extreme that they name: Within the 4 slots of one device the pairs (tile_rows, tile_cols) are distinct. Within the 4 slots of one device the pairs (tile_rows, tile_cols) are distinct. A slot with kept_counts 0 is empty, and empty slots come after all live slots of a device; a live slot keeps 512 // 2 or more coefficients; every device has a live slot, and some device has all 4 slots live.
All inputs are finite; a program needn't handle non-finite values.
Results may differ from a plain program's by a relative error of at most 0.033.
Values may be sent and summed in bfloat16 or wider, within the bound.
No kernel may reach another device: no remote copies, remote signals or barrier semaphores. Data moves between devices by JAX's collectives and lax.ppermute only.
A program may use at most 64 MiB of HBM per device.

v0:
```python
import math

import jax
import jax.numpy as jnp
from jax import lax
from jax.sharding import PartitionSpec as P

ITERS = 4


damping = 1.0


def haar_matrix(tile_size):
    rows_index = jnp.arange(tile_size, dtype=jnp.int32)[:, None]
    column_index = jnp.arange(tile_size, dtype=jnp.int32)[None, :]
    levels = jnp.zeros_like(rows_index)
    for bit_shift in range(1, tile_size.bit_length()):
        levels = levels + (rows_index >= 1 << bit_shift).astype(jnp.int32)
    support = jnp.right_shift(tile_size, levels)
    offset = (rows_index - jnp.left_shift(1, levels)) * support
    inside = (column_index >= offset) & (column_index < offset + support)
    polarity = jnp.where(column_index < offset + support // 2, 1.0, -1.0)
    detail = jnp.where(inside, polarity, 0.0) / jnp.sqrt(support.astype(jnp.float32))
    coarse = jnp.full((1, tile_size), 1.0 / math.sqrt(tile_size), jnp.float32)
    return jnp.concatenate([coarse, detail[1:]], axis=0)


def squared_norm(values):
    return lax.psum(jnp.sum(values * values), "cols")


def per_device(
    sensitivity, tile_rows, tile_cols, kept_counts, misfit, data_weight, depth_weight, density
):
    tile_stack = sensitivity[0]
    slot_rows = tile_rows[0]
    slot_cols = tile_cols[0]
    slot_kept = kept_counts[0]
    tile_size = tile_stack.shape[-1]
    data_blocks = misfit.shape[0] // tile_size
    model_blocks = density.shape[0] // tile_size
    wavelet = haar_matrix(tile_size)
    coefficient_index = jnp.arange(tile_size, dtype=jnp.int32)
    live_mask = coefficient_index[None, :] < slot_kept[:, None]
    pick_rows = slot_rows[:, None] == jnp.arange(data_blocks, dtype=jnp.int32)[None, :]
    pick_cols = slot_cols[:, None] == jnp.arange(model_blocks, dtype=jnp.int32)[None, :]
    share_len = misfit.shape[0] // lax.axis_size("cols")
    share_start = lax.axis_index("cols") * share_len
    squared = data_weight * data_weight

    def adjoint_part(weighted):
        data_rows = weighted.reshape(data_blocks, tile_size)
        picked = jnp.dot(
            pick_rows.astype(jnp.bfloat16), data_rows, preferred_element_type=jnp.float32
        ).astype(jnp.bfloat16)
        products = jnp.einsum("sab,sa->sb", tile_stack, picked, preferred_element_type=jnp.float32)
        products = jnp.where(live_mask, products, 0.0)
        block_sums = jnp.dot(
            pick_cols.T.astype(jnp.float32), products, precision=lax.Precision.HIGHEST
        )
        cell_part = jnp.dot(block_sums, wavelet, precision=lax.Precision.HIGHEST).reshape(-1)
        return lax.psum(cell_part, "rows")

    rhs = depth_weight * adjoint_part((squared * misfit).astype(jnp.bfloat16)) - damping * density
    solution = jnp.zeros_like(density)
    residual = rhs
    direction = rhs
    norm_now = squared_norm(residual)
    change = jnp.zeros_like(misfit)
    for iteration in range(ITERS):
        coeffs = jnp.dot(
            (depth_weight * direction).reshape(model_blocks, tile_size),
            wavelet.T,
            precision=lax.Precision.HIGHEST,
        )
        forward_picked = jnp.dot(
            pick_cols.astype(jnp.float32), coeffs, precision=lax.Precision.HIGHEST
        )
        forward_picked = jnp.where(live_mask, forward_picked, 0.0).astype(jnp.bfloat16)
        forward_products = jnp.einsum(
            "sab,sb->sa", tile_stack, forward_picked, preferred_element_type=jnp.float32
        )
        summed = jnp.dot(
            pick_rows.T.astype(jnp.float32), forward_products, precision=lax.Precision.HIGHEST
        )
        partial_data = summed.reshape(-1)
        image_data = lax.psum(partial_data, "cols")
        weighted = (squared * image_data).astype(jnp.bfloat16)
        image_cells = depth_weight * adjoint_part(weighted) + damping * direction
        curvature_sum = lax.psum(jnp.sum(direction * image_cells), "cols")
        step_length = norm_now / curvature_sum
        solution = solution + step_length * direction
        residual = residual - step_length * image_cells
        change = change + step_length * image_data
        if iteration + 1 < ITERS:
            norm_next = squared_norm(residual)
            direction = residual + norm_next / norm_now * direction
            norm_now = norm_next
    new_density = density + depth_weight * solution
    new_misfit = lax.dynamic_slice_in_dim(misfit - change, share_start, share_len)
    return (new_density, new_misfit)


def solution(mesh):
    return jax.shard_map(
        per_device,
        mesh=mesh,
        in_specs=(
            P("rows", "cols", None, None),
            P("rows", "cols"),
            P("rows", "cols"),
            P("rows", "cols"),
            P("rows"),
            P("rows"),
            P("cols"),
            P("cols"),
        ),
        out_specs=(P("cols"), P(("rows", "cols"))),
        check_vma=False,
    )
```

profile of v0, /device:TPU:1, one launch (start us, length us, event | category | flops | bytes accessed | tf_op | source)
XLA Modules:
  0.0 1661.8 jit_solution(10881890196141592567)
XLA Ops:
  7.3 1.2 multiply_convert_fusion.4
  11.4 9.5 psum.119
  21.0 0.9 fusion.42
  24.1 178.2 %all-reduce.7.cloned.1.call-done = f32[65536]{0:T(1024)} async-done(((f32[65536]{0:T(1024)}), f32[65536]{0:T(1024)}) %all-reduce.7.cloned.1.call-update) | async-done | bytes 262160 | tf_op jit(solution)/shard_map/psum | solution.py:88
  202.3 1.0 multiply_convert_fusion.3
  204.0 1.1 fusion.23
  205.5 0.9 fusion.51
  207.1 8.4 psum.122
  216.2 125.2 %all-reduce.1 = (f32[]{:T(128)}, f32[]{:T(128)}) all-reduce(f32[]{:T(128)} %get-tuple-element.3, f32[]{:T(128)} %get-tuple-element.2), channel_id=1, replica_groups=mesh['rows'=4,'cols'=64] {'cols'}, use_global_device_ids=true, to_apply=%region_2.3 | all-reduce | flops 2 | bytes 16 | tf_op jit(solution)/shard_map/psum | solution.py:30
  343.3 124.8 %psum.124 = f32[]{:T(128)} all-reduce(f32[]{:T(128)} %multiply_reduce_fusion.4), channel_id=1, replica_groups=mesh['rows'=4,'cols'=64] {'cols'}, use_global_device_ids=true, to_apply=%region_8.9 | all-reduce | flops 1 | bytes 8 | tf_op jit(solution)/shard_map/psum | solution.py:30
  469.5 0.9 fusion.39
  472.5 167.1 %all-reduce.9.cloned.1.call-done = f32[65536]{0:T(1024)} async-done(((f32[65536]{0:T(1024)}), f32[65536]{0:T(1024)}) %all-reduce.9.cloned.1.call-update) | async-done | bytes 262160 | tf_op jit(solution)/shard_map/psum | solution.py:88
  639.6 1.0 multiply_convert_fusion.2
  641.4 1.1 fusion.24
  642.8 0.9 fusion.49
  644.5 8.4 psum.126
  653.5 125.2 %psum.127 = f32[]{:T(128)} all-reduce(f32[]{:T(128)} %multiply_reduce_fusion.3), channel_id=1, replica_groups=mesh['rows'=4,'cols'=64] {'cols'}, use_global_device_ids=true, to_apply=%region_12.13 | all-reduce | flops 1 | bytes 8 | tf_op jit(solution)/shard_map/psum | solution.py:91
  780.6 124.8 %psum.128 = f32[]{:T(128)} all-reduce(f32[]{:T(128)} %get-tuple-element.8), channel_id=1, replica_groups=mesh['rows'=4,'cols'=64] {'cols'}, use_global_device_ids=true, to_apply=%region_14.15 | all-reduce | flops 1 | bytes 8 | tf_op jit(solution)/shard_map/psum | solution.py:30
  906.8 0.9 fusion.36
  909.9 167.0 %all-reduce.11.cloned.1.call-done = f32[65536]{0:T(1024)} async-done(((f32[65536]{0:T(1024)}), f32[65536]{0:T(1024)}) %all-reduce.11.cloned.1.call-update) | async-done | bytes 262160 | tf_op jit(solution)/shard_map/psum | solution.py:88
  1076.9 1.0 multiply_convert_fusion.1
  1078.7 1.1 fusion.25
  1081.2 8.4 psum.130
  1090.3 125.1 %psum.131 = f32[]{:T(128)} all-reduce(f32[]{:T(128)} %multiply_reduce_fusion.1), channel_id=1, replica_groups=mesh['rows'=4,'cols'=64] {'cols'}, use_global_device_ids=true, to_apply=%region_18.19 | all-reduce | flops 1 | bytes 8 | tf_op jit(solution)/shard_map/psum | solution.py:91
  1217.4 124.6 %psum.132 = f32[]{:T(128)} all-reduce(f32[]{:T(128)} %multiply_reduce_fusion), channel_id=1, replica_groups=mesh['rows'=4,'cols'=64] {'cols'}, use_global_device_ids=true, to_apply=%region_20.21 | all-reduce | flops 1 | bytes 8 | tf_op jit(solution)/shard_map/psum | solution.py:30
  1346.5 167.2 %all-reduce.13.cloned.1.call-done = f32[65536]{0:T(1024)} async-done(((f32[65536]{0:T(1024)}), f32[65536]{0:T(1024)}) %all-reduce.13.cloned.1.call-update) | async-done | bytes 262160 | tf_op jit(solution)/shard_map/psum | solution.py:88
  1513.6 1.0 multiply_convert_fusion
  1515.9 0.9 fusion.45
  1517.6 8.4 psum.134
  1526.0 1.4 fusion.72
  1527.4 125.2 %psum.135 = f32[]{:T(128)} all-reduce(f32[]{:T(128)} %fusion.72), channel_id=1, replica_groups=mesh['rows'=4,'cols'=64] {'cols'}, use_global_device_ids=true, to_apply=%region_24.25 | all-reduce | flops 1 | bytes 8 | tf_op jit(solution)/shard_map/psum | solution.py:91
  1653.9 1.4 dynamic-slice_subtract_fusion
  (108 shorter events, 23.8 us)
Async XLA Ops:
  7.2 2.6 copy-start
  7.2 2.9 copy-start.14
  7.2 2.9 copy-start.10
  7.2 195.1 %all-reduce.7.cloned.1.call-start = ((), (), s32[]{:S(2)}) async-start(), calls=%async_computation | async-start | bytes 524288 | tf_op jit(solution)/shard_map/psum | solution.py:88
  9.7 11.3 copy-start.2
  9.7 11.3 copy-start.6
  10.8 12.1 copy-start.7
  21.0 181.3 %copy-start.1 = (f32[65536]{0:T(1024)S(1)}, f32[65536]{0:T(1024)}, u32[]{:S(2)}) copy-start(f32[65536]{0:T(1024)} %param.13) | copy-start | bytes 786436
  24.0 615.6 %all-reduce.9.cloned.1.call-start = ((), (), s32[]{:S(2)}) async-start(), calls=%async_computation.1 | async-start | bytes 524288 | tf_op jit(solution)/shard_map/psum | solution.py:88
  205.1 265.3 %copy-start.11 = (s32[1,4]{1,0:T(1,128)S(1)}, s32[1,4]{1,0:T(1,128)}, u32[]{:S(2)}) copy-start(s32[1,4]{1,0:T(1,128)} %param.11) | copy-start | bytes 52
  205.1 265.3 %copy-start.15 = (s32[1,4]{1,0:T(1,128)S(1)}, s32[1,4]{1,0:T(1,128)}, u32[]{:S(2)}) copy-start(s32[1,4]{1,0:T(1,128)} %param.10) | copy-start | bytes 52
  472.5 604.5 %all-reduce.11.cloned.1.call-start = ((), (), s32[]{:S(2)}) async-start(), calls=%async_computation.2 | async-start | bytes 524288 | tf_op jit(solution)/shard_map/psum | solution.py:88
  642.4 265.3 %copy-start.12 = (s32[1,4]{1,0:T(1,128)S(1)}, s32[1,4]{1,0:T(1,128)}, u32[]{:S(2)}) copy-start(s32[1,4]{1,0:T(1,128)} %param.11) | copy-start | bytes 52
  642.5 265.3 %copy-start.16 = (s32[1,4]{1,0:T(1,128)S(1)}, s32[1,4]{1,0:T(1,128)}, u32[]{:S(2)}) copy-start(s32[1,4]{1,0:T(1,128)} %param.10) | copy-start | bytes 52
  643.8 264.9 %copy-start.8 = (s32[1,4]{1,0:T(1,128)S(1)}, s32[1,4]{1,0:T(1,128)}, u32[]{:S(2)}) copy-start(s32[1,4]{1,0:T(1,128)} %param.9) | copy-start | bytes 52
  780.6 129.2 %copy-start.3 = (f32[1024]{0:T(1024)}, f32[1024]{0:T(1024)S(1)}, u32[]{:S(2)}) copy-start(f32[1024]{0:T(1024)S(1)} %get-tuple-element.9) | copy-start | bytes 12292
  909.9 603.8 %all-reduce.13.cloned.1.call-start = ((), (), s32[]{:S(2)}) async-start(), calls=%async_computation.3 | async-start | bytes 524288 | tf_op jit(solution)/shard_map/psum | solution.py:88
  1078.7 1.5 copy-start.13
  1078.7 1.5 copy-start.17
  1078.7 138.1 %copy-start.4 = (f32[1024]{0:T(1024)S(1)}, f32[1024]{0:T(1024)}, u32[]{:S(2)}) copy-start(f32[1024]{0:T(1024)} %copy-done.3) | copy-start | bytes 12292
  1080.5 264.8 %copy-start.9 = (s32[1,4]{1,0:T(1,128)S(1)}, s32[1,4]{1,0:T(1,128)}, u32[]{:S(2)}) copy-start(s32[1,4]{1,0:T(1,128)} %param.9) | copy-start | bytes 52
  1089.6 256.9 %copy-start.5 = (f32[1024]{0:T(1024)}, f32[1024]{0:T(1024)S(1)}, u32[]{:S(2)}) copy-start(f32[1024]{0:T(1024)S(1)} %psum.130) | copy-start | bytes 12292
Sparse Core Ops, SparseCore 0:
  24.2 178.0 all-reduce.6
  472.6 166.9 all-reduce.8
  910.0 166.9 all-reduce.10
  1346.6 167.0 all-reduce.12
where the time goes:
time: 1660 us
  blocking collectives  918 us (55%)
  waiting for transfers between devices  680 us (41%)
  between operations  23.4 us (1%)
  matrix products  22.4 us (1%)
    psum x4, waiting for transfers between devices, per_device(): image_data = lax.psum(partial_data, 'cols')  679 us
    psum x4, blocking collectives, squared_norm(): return lax.psum(jnp.sum(values * values), 'cols')  499 us
    psum x3, blocking collectives, per_device(): curvature_sum = lax.psum(jnp.sum(direction * image_cells), 'cols')  376 us
    psum x5, blocking collectives, adjoint_part(): return lax.psum(cell_part, 'rows')  43.3 us
  transfers between devices with their start and end apart: 4, of which 4 were waited for; matrix products, arithmetic and copies ran while one was open for 0% of the time, Pallas kernels for 0%

commit v1 on v0

v1 whole, which is shorter than its diff:
```python
import functools
import math

import jax
import jax.numpy as jnp
from jax import lax
from jax.experimental import pallas as pl
from jax.experimental.pallas import tpu as pltpu
from jax.sharding import Mesh, PartitionSpec as P

ITERS = 4
LANES = 128
SLOTS = 4
TILE = 512
CHUNKS = TILE // LANES
PRODUCT_ROWS = SLOTS * CHUNKS
MESSAGE_ROWS = PRODUCT_ROWS + 8

damping = 1.0

NN = (((1,), (0,)), ((), ()))
NT = (((1,), (1,)), ((), ()))


def haar_signs(size):
    row = lax.broadcasted_iota(jnp.int32, (size, size), 0)
    column = lax.broadcasted_iota(jnp.int32, (size, size), 1)
    level = haar_levels(row, size)
    shift = size.bit_length() - 1 - level
    place = column - jnp.left_shift(row - jnp.left_shift(1, level), shift)
    support = jnp.left_shift(1, shift)
    signs = jnp.where(place < jnp.right_shift(support, 1), 1.0, -1.0)
    signs = jnp.where((place >= 0) & (place < support), signs, 0.0)
    return jnp.where(row == 0, 1.0, signs).astype(jnp.bfloat16)


def haar_levels(row, size):
    level = jnp.zeros_like(row)
    for bit in range(1, size.bit_length() - 1):
        level = level + (row >= 1 << bit).astype(jnp.int32)
    return level


def haar_scales(size):
    row = lax.broadcasted_iota(jnp.int32, (1, size), 1)
    scales = jnp.full((1, size), 1.0 / math.sqrt(size), jnp.float32)
    for bit in range(1, size.bit_length() - 1):
        scales = jnp.where(row >= 1 << bit, math.sqrt((1 << bit) / size), scales)
    return scales


def matmul(a, b, dims):
    return lax.dot_general(a, b, dims, preferred_element_type=jnp.float32)


def split3(value):
    high = value.astype(jnp.bfloat16).astype(jnp.float32)
    rest = value - high
    middle = rest.astype(jnp.bfloat16).astype(jnp.float32)
    low = (rest - middle).astype(jnp.bfloat16).astype(jnp.float32)
    return high, middle, low


def total(values):
    return jnp.sum(jnp.sum(values, axis=0, keepdims=True), axis=1, keepdims=True)


def to_lanes(values):
    blocks = values.shape[0] // CHUNKS
    return jnp.concatenate(
        [
            jnp.concatenate(
                [values[CHUNKS * b + k : CHUNKS * b + k + 1] for k in range(CHUNKS)], axis=1
            )
            for b in range(blocks)
        ],
        axis=0,
    )


def to_rows(values):
    return jnp.concatenate(
        [
            values[b : b + 1, LANES * k : LANES * (k + 1)]
            for b in range(values.shape[0])
            for k in range(CHUNKS)
        ],
        axis=0,
    )


def times_haar(vectors, signs_ref, dims):
    parts = jnp.concatenate(split3(vectors) + (jnp.zeros((10, TILE), jnp.float32),), axis=0)
    product = matmul(parts.astype(jnp.bfloat16), signs_ref[...], dims)
    return product[0:2] + product[2:4] + product[4:6]


def slot_products(vectors, tiles_ref, dims):
    row = lax.broadcasted_iota(jnp.int32, (16, TILE), 0)
    out = jnp.zeros((16, TILE), jnp.float32)
    for s in range(SLOTS):
        out = jnp.where(row == s, matmul(vectors, tiles_ref[s], dims), out)
    return out


def adjoint(picked, masks, tiles_ref, signs_ref):
    vectors = jnp.concatenate([picked, jnp.zeros((12, TILE), jnp.float32)], axis=0)
    products = slot_products(vectors.astype(jnp.bfloat16), tiles_ref, NN)[0:SLOTS]
    sums = [
        jnp.sum(masks[SLOTS * m : SLOTS * (m + 1)] * products, axis=0, keepdims=True)
        for m in range(2)
    ]
    sums = jnp.concatenate(sums, axis=0) * haar_scales(TILE)
    return to_rows(times_haar(sums, signs_ref, NN))


def forward_message(cells, residual, direction, masks_ref, ids_ref, tiles_ref, signs_ref,
                    message_ref):
    coeffs = times_haar(to_lanes(cells), signs_ref, NT) * haar_scales(TILE)
    picked = masks_ref[0:SLOTS, :] * coeffs[0:1] + masks_ref[SLOTS : 2 * SLOTS, :] * coeffs[1:2]
    picked = jnp.concatenate([picked, jnp.zeros((12, TILE), jnp.float32)], axis=0)
    products = slot_products(picked.astype(jnp.bfloat16), tiles_ref, NT)
    norm = split3(jnp.sum(residual * residual, axis=0, keepdims=True))
    cross = split3(jnp.sum(residual * direction, axis=0, keepdims=True))
    pieces = [products[0:SLOTS, LANES * k : LANES * (k + 1)] for k in range(CHUNKS)]
    pieces += list(norm) + list(cross) + [ids_ref[0:2, :]]
    message = jnp.concatenate(pieces, axis=0).astype(jnp.bfloat16)
    message_ref[...] = jnp.broadcast_to(message[None], message_ref.shape)


def my_column():
    plane = lax.axis_index("x") * lax.axis_size("z") + lax.axis_index("z")
    return plane * lax.axis_size("core") + lax.axis_index("core")


def first_adjoint_kernel(slots_ref, weighted_ref, tiles_ref, signs_ref, part_ref, masks_ref, ids_ref,
                         pick_ref):
    rows = [slots_ref[0, s] for s in range(SLOTS)]
    column = lax.broadcasted_iota(jnp.int32, (1, TILE), 1)
    masks = jnp.concatenate(
        [
            (
                column < jnp.where(slots_ref[0, SLOTS + s] == m, slots_ref[0, 2 * SLOTS + s], 0)
            ).astype(jnp.float32)
            for m in range(2)
            for s in range(SLOTS)
        ],
        axis=0,
    )
    masks_ref[...] = masks
    picked = jnp.concatenate(
        [to_lanes(weighted_ref[pl.ds(row * CHUNKS, CHUNKS), :]) for row in rows], axis=0
    )
    part_ref[...] = adjoint(picked, masks, tiles_ref, signs_ref)
    lane = lax.broadcasted_iota(jnp.int32, (1, LANES), 1)
    row_ids = jnp.zeros((1, LANES), jnp.int32)
    for u in range(2 * SLOTS):
        row_ids = jnp.where(lane == u, rows[u % SLOTS] + (u // SLOTS) * LANES, row_ids)
    ids_ref[...] = jnp.broadcast_to(row_ids.astype(jnp.float32), ids_ref.shape)
    wide = lax.broadcasted_iota(jnp.int32, (1, 2 * LANES), 1)
    picks = [(wide == row + p * LANES).astype(jnp.float32) for p in range(2) for row in rows]
    pick_ref[...] = jnp.concatenate(
        picks + [jnp.zeros((8, 2 * LANES), jnp.float32)], axis=0
    ).astype(jnp.bfloat16)


def first_forward_kernel(masks_ref, ids_ref, tiles_ref, signs_ref, depth_ref, density_ref,
                         part0_ref, part1_ref, part2_ref, part3_ref, message_ref, residual_ref):
    sums = (part0_ref[...] + part2_ref[...]) + (part1_ref[...] + part3_ref[...])
    residual = depth_ref[...] * sums - damping * density_ref[...]
    residual_ref[...] = residual
    forward_message(depth_ref[...] * residual, residual, jnp.zeros_like(residual), masks_ref, ids_ref,
                    tiles_ref, signs_ref, message_ref)


def gathered(ref):
    values = ref[...].astype(jnp.float32)
    wide = ref.shape[0] * 8
    half = jnp.concatenate(
        [values[:, 8 * j : 8 * j + 8, :].reshape(wide, LANES) for j in range(2)], axis=1
    )
    return half.astype(jnp.bfloat16), values[:, PRODUCT_ROWS:, :]


def data_block_ids(tail):
    planes = tail.shape[0]
    wide = planes * 8
    pick = (
        lax.broadcasted_iota(jnp.int32, (16, LANES), 1)
        == lax.broadcasted_iota(jnp.int32, (16, LANES), 0)
    ).astype(jnp.bfloat16)
    spread = (
        lax.broadcasted_iota(jnp.int32, (planes, wide), 1) // 8
        == lax.broadcasted_iota(jnp.int32, (planes, wide), 0)
    ).astype(jnp.bfloat16)
    mine = lax.broadcasted_iota(jnp.int32, (16, wide), 1) % 8
    mine = mine == lax.broadcasted_iota(jnp.int32, (16, wide), 0)
    held = jnp.sum(tail[:, 6:7, :], axis=1).astype(jnp.bfloat16)
    turned = matmul(pick, held, NT).astype(jnp.bfloat16)
    return jnp.sum(jnp.where(mine, matmul(turned, spread, NN), 0.0), axis=0, keepdims=True)


def summed_field(ids, halves):
    wide = halves[0].shape[0]
    index = lax.broadcasted_iota(jnp.int32, (2 * LANES, wide), 0).astype(jnp.float32)
    return matmul((index == ids[0]).astype(jnp.bfloat16), halves[0], NN) + matmul(
        (index == ids[1]).astype(jnp.bfloat16), halves[1], NN
    )


def write_cells(cells_out_ref, direction, norm_now, direction_norm, field_ref):
    cells_out_ref[0:8, :] = direction
    cells_out_ref[8:16, :] = jnp.broadcast_to(norm_now, (8, LANES))
    cells_out_ref[16:24, :] = jnp.broadcast_to(direction_norm, (8, LANES))
    column = my_column()
    share = []
    for b in range(2):
        rows = [field_ref[pl.ds(p * LANES + 2 * column + b, 1), :] for p in range(2)]
        share += [rows[k % 2][:, LANES * (k // 2) : LANES * (k // 2 + 1)] for k in range(CHUNKS)]
    cells_out_ref[24:32, :] = jnp.concatenate(share, axis=0)


def weigh(squared, field):
    weighted = (squared * field).astype(jnp.bfloat16)
    norm = jnp.sum(
        (weighted.astype(jnp.float32) * field).reshape(2 * LANES // 8, 8, 2 * LANES), axis=0
    )
    return weighted, norm[:, :LANES] + norm[:, LANES:]


def slot_blocks(pick_ref, weighted):
    picked = matmul(pick_ref[...], weighted, NN)
    return jnp.concatenate(
        [
            picked[SLOTS * (k % 2) : SLOTS * (k % 2 + 1), LANES * (k // 2) : LANES * (k // 2 + 1)]
            for k in range(CHUNKS)
        ],
        axis=1,
    )


def first_data_kernel(masks_ref, pick_ref, tiles_ref, signs_ref, weight_ref, residual_ref,
                      own_ref, other_ref, part_ref, cells_out_ref, field_ref, ids_ref, squared_ref):
    halves, tails = zip(*(gathered(ref) for ref in (own_ref, other_ref)))
    sums = jnp.sum(tails[0] + tails[1], axis=0)
    norm_now = total(sums[0:3])
    ids = [data_block_ids(tail) for tail in tails]
    for n in range(2):
        ids_ref[n : n + 1, :] = ids[n]
    field = summed_field(ids, halves)
    field_ref[...] = field
    weight = jnp.concatenate(
        [
            jnp.concatenate(
                [weight_ref[pl.ds(2 * j + p, LANES, stride=CHUNKS), :] for j in range(2)], axis=1
            )
            for p in range(2)
        ],
        axis=0,
    )
    squared = weight * weight
    squared_ref[...] = squared
    weighted, norm_part = weigh(squared, field)
    part_ref[0:8, :] = adjoint(
        slot_blocks(pick_ref, weighted), masks_ref[...], tiles_ref, signs_ref
    )
    part_ref[8:16, :] = norm_part
    write_cells(cells_out_ref, residual_ref[...], norm_now, norm_now, field_ref)


def next_field(residual_ref, cells_ref, field_in_ref, ids_ref, own_ref, other_ref):
    halves, tails = zip(*(gathered(ref) for ref in (own_ref, other_ref)))
    sums = jnp.sum(tails[0] + tails[1], axis=0)
    norm_now = total(sums[0:3])
    cross = total(sums[3:6])
    ratio = norm_now / cells_ref[8:9, 0:1]
    field = summed_field([ids_ref[0:1, :], ids_ref[1:2, :]], halves) + ratio * field_in_ref[...]
    direction = residual_ref[0:8, :] + ratio * cells_ref[0:8, :]
    direction_norm = norm_now + ratio * (2.0 * cross + ratio * cells_ref[16:17, 0:1])
    return field, direction, norm_now, direction_norm


def data_kernel(masks_ref, pick_ref, tiles_ref, signs_ref, squared_ref, residual_ref,
                cells_ref, field_in_ref, ids_ref, own_ref, other_ref, part_ref, cells_out_ref,
                field_ref):
    field, direction, norm_now, direction_norm = next_field(
        residual_ref, cells_ref, field_in_ref, ids_ref, own_ref, other_ref
    )
    field_ref[...] = field
    weighted, norm_part = weigh(squared_ref[...], field)
    part_ref[0:8, :] = adjoint(
        slot_blocks(pick_ref, weighted), masks_ref[...], tiles_ref, signs_ref
    )
    part_ref[8:16, :] = norm_part
    write_cells(cells_out_ref, direction, norm_now, direction_norm, field_ref)


def last_data_kernel(squared_ref, residual_ref, cells_ref, field_in_ref, ids_ref, own_ref, other_ref,
                     part_ref, cells_out_ref, field_ref):
    field, direction, norm_now, direction_norm = next_field(
        residual_ref, cells_ref, field_in_ref, ids_ref, own_ref, other_ref
    )
    field_ref[...] = field
    part_ref[...] = weigh(squared_ref[...], field)[1]
    write_cells(cells_out_ref, direction, norm_now, direction_norm, field_ref)


def step_kernel(started, masks_ref, ids_ref, tiles_ref, signs_ref, depth_ref, cells_ref,
                state_ref, part0_ref, part1_ref, part2_ref, part3_ref, message_ref, state_out_ref):
    sums = (part0_ref[...] + part2_ref[...]) + (part1_ref[...] + part3_ref[...])
    direction = cells_ref[0:8, :]
    length = cells_ref[8:9, 0:1] / (total(sums[8:16]) + damping * cells_ref[16:17, 0:1])
    image = depth_ref[...] * sums[0:8] + damping * direction
    residual = state_ref[0:8, :] - length * image
    solution = length * direction
    change = length * cells_ref[24:32, :]
    if started:
        solution = state_ref[8:16, :] + solution
        change = state_ref[16:24, :] + change
    state_out_ref[0:8, :] = residual
    state_out_ref[8:16, :] = solution
    state_out_ref[16:24, :] = change
    forward_message(depth_ref[...] * residual, residual, direction, masks_ref, ids_ref, tiles_ref,
                    signs_ref, message_ref)


def last_kernel(depth_ref, density_ref, misfit_ref, cells_ref, state_ref, part0_ref, part1_ref,
                part2_ref, part3_ref, density_out_ref, misfit_out_ref):
    sums = (part0_ref[...] + part2_ref[...]) + (part1_ref[...] + part3_ref[...])
    length = cells_ref[8:9, 0:1] / (total(sums) + damping * cells_ref[16:17, 0:1])
    solution = state_ref[8:16, :] + length * cells_ref[0:8, :]
    density_out_ref[...] = density_ref[...] + depth_ref[...] * solution
    misfit_out_ref[...] = misfit_ref[...] - (state_ref[16:24, :] + length * cells_ref[24:32, :])


def shifts_along_rows(values):
    n = lax.axis_size("rows")
    opposite, left, right = (
        lax.ppermute(values, "rows", [(i, (i + step) % n) for i in range(n)]) for step in (2, 1, 3)
    )
    return values, left, opposite, right


def exchange(message):
    own = lax.all_to_all(message, ("x", "z"), 0, 0)
    return own, lax.ppermute(own, "core", [(0, 1), (1, 0)])


def call(kernel, out_shape, operands, scratch=()):
    spaces = [
        pltpu.VMEM if jnp.issubdtype(a.dtype, jnp.floating) else pltpu.SMEM for a in operands
    ]
    return pl.pallas_call(
        kernel,
        out_shape=out_shape,
        in_specs=[pl.BlockSpec(memory_space=space) for space in spaces],
        out_specs=jax.tree.map(lambda _: pl.BlockSpec(memory_space=pltpu.VMEM), out_shape),
        scratch_shapes=list(scratch),
        compiler_params=pltpu.CompilerParams(vmem_limit_bytes=24 * 2**20),
    )(*operands)


def per_device(
    sensitivity, tile_rows, tile_cols, kept_counts, misfit, data_weight, depth_weight, density
):
    tiles = sensitivity[0]
    signs = haar_signs(TILE)
    slots = jnp.concatenate([tile_rows, tile_cols, kept_counts], axis=1)
    misfit, data_weight, depth, density = (
        a.reshape(-1, LANES) for a in (misfit, data_weight, depth_weight, density)
    )
    own_misfit = lax.dynamic_slice_in_dim(misfit, my_column() * 8, 8)
    planes = lax.axis_size("x") * lax.axis_size("z")
    f32 = functools.partial(jax.ShapeDtypeStruct, dtype=jnp.float32)
    cells_shape = f32((8, LANES))
    message_shape = jax.ShapeDtypeStruct((planes, MESSAGE_ROWS, LANES), jnp.bfloat16)
    field_shape = f32((2 * LANES, 2 * LANES))
    pick_shape = jax.ShapeDtypeStruct((16, 2 * LANES), jnp.bfloat16)

    part, masks, row_ids, pick = call(
        first_adjoint_kernel,
        (cells_shape, f32((8, TILE)), cells_shape, pick_shape),
        (slots, data_weight * data_weight * misfit, tiles, signs),
    )
    forward_with = (masks, row_ids, tiles, signs)
    adjoint_with = (masks, pick, tiles, signs)
    message, state = call(
        first_forward_kernel,
        (message_shape, cells_shape),
        forward_with + (depth, density) + shifts_along_rows(part),
    )
    part, cells, field, ids, squared = call(
        first_data_kernel,
        (f32((16, LANES)), f32((32, LANES)), field_shape, f32((8, planes * 8)), field_shape),
        adjoint_with + (data_weight, state) + exchange(message),
    )
    for iteration in range(1, ITERS):
        message, state = call(
            functools.partial(step_kernel, iteration > 1),
            (message_shape, f32((24, LANES))),
            forward_with + (depth, cells, state) + shifts_along_rows(part),
        )
        carried = (squared, state, cells, field, ids) + exchange(message)
        if iteration + 1 < ITERS:
            part, cells, field = call(
                data_kernel,
                (f32((16, LANES)), f32((32, LANES)), field_shape),
                adjoint_with + carried,
            )
    part, cells = call(
        last_data_kernel,
        (cells_shape, f32((32, LANES))),
        carried,
        [pltpu.VMEM(field_shape.shape, jnp.float32)],
    )
    new_density, new_misfit = call(
        last_kernel,
        (cells_shape, cells_shape),
        (depth, density, own_misfit, cells, state) + shifts_along_rows(part),
    )
    return (new_density.reshape(-1), new_misfit.reshape(-1))


def solution(mesh):
    cols = ("x", "z", "core")
    fine = Mesh(mesh.devices.reshape(4, 4, 8, 2), ("rows",) + cols)
    return jax.shard_map(
        per_device,
        mesh=fine,
        in_specs=(
            P("rows", cols, None, None),
            P("rows", cols),
            P("rows", cols),
            P("rows", cols),
            P("rows"),
            P("rows"),
            P(cols),
            P(cols),
        ),
        out_specs=(P(cols), P(("rows",) + cols)),
        check_vma=False,
    )
```

time: 1660 us -> 123 us (0.07)
  blocking collectives: 918 us -> 58.9 us
  waiting for transfers between devices: 680 us -> 14.9 us
  starting transfers between devices: 0.16 us -> 34 us
  between operations: 23.4 us -> 0.79 us
  matrix products: 22.4 us -> 0 us
    psum x12 -> x0, blocking collectives: 918 us -> none  [the longest x4 499 us: squared_norm(): return lax.psum(jnp.sum(values * values), 'cols')]
    psum x4 -> x0, waiting for transfers between devices: 679 us -> none  [per_device(): image_data = lax.psum(partial_data, 'cols')]
    all_to_all x0 -> x4, blocking collectives: none -> 58.9 us  [exchange(): own = lax.all_to_all(message, ('x', 'z'), 0, 0)]
    ppermute x0 -> x19, starting transfers between devices: none -> 34 us  [the longest x15 18.9 us: shifts_along_rows(): lax.ppermute(values, 'rows', [(i, (i + step) % n) for i in range(n)])]
    dot_general x36 -> x0, matrix products: 22.4 us -> none  [the longest x5 5 us: adjoint_part(): jnp.dot(pick_rows.astype(jnp.bfloat16), data_rows, preferred_element_type...]
  transfers between devices with their start and end apart: 4 -> 19, of which waited for: 4 -> 16; matrix products, arithmetic and copies ran while one was open for 0% -> 1% of each run, Pallas kernels for 0% -> 0%
where the time goes in v1:
time: 123 us; the launch traced here: 122 us
  blocking collectives  58.9 us (48%)
  starting transfers between devices  34 us (28%)
  waiting for transfers between devices  14.9 us (12%)
  Pallas kernels  9.03 us (7%)
  other arithmetic  2.47 us (2%)
  local copies, waits for them, and re-layouts  2.3 us (2%)
    all_to_all x4, blocking collectives, exchange(): own = lax.all_to_all(message, ('x', 'z'), 0, 0)  58.9 us
    ppermute x15, starting transfers between devices, shifts_along_rows(): lax.ppermute(values, 'rows', [(i, (i + step) % n) for i in range(n)])  18.9 us
    ppermute x4, starting transfers between devices, exchange(): return (own, lax.ppermute(own, 'core', [(0, 1), (1, 0)]))  15.1 us
    ppermute x15, waiting for transfers between devices, shifts_along_rows(): lax.ppermute(values, 'rows', [(i, (i + step) % n) for i in range(n)])  10.6 us
    pallas_call x10, Pallas kernels, call(): pl.pallas_call(kernel, out_shape=out_shape, in_specs=[pl.BlockSpec(memory...  9.03 us
    ppermute x4, waiting for transfers between devices, exchange(): return (own, lax.ppermute(own, 'core', [(0, 1), (1, 0)]))  4.28 us
  transfers between devices with their start and end apart: 19, of which 16 were waited for; matrix products, arithmetic and copies ran while one was open for 1% of the time, Pallas kernels for 0%

profile of v1, /device:TPU:1, one launch (start us, length us, event | category | flops | bytes accessed | tf_op | source)
XLA Modules:
  0.0 122.4 jit_solution(14295648752439898674)
XLA Ops:
  0.7 1.1 multiply_multiply_fusion.weighted_ref
  3.2 1.6 %copy-done = bf16[1,4,512,512]{3,2,1,0:T(8,128)(2,1)S(1)} copy-done((bf16[1,4,512,512]{3,2,1,0:T(8,128)(2,1)S(1)}, bf16[1,4,512,512]{3,2,1,0:T(8,128)(2,1)}, u32[]{:S(2)}) %copy-start) | copy-done | bytes 2097176
  4.7 1.1 shard_map.95
  5.9 2.2 %collective-permute-start = (f32[8,128]{1,0:T(8,128)S(1)}, f32[8,128]{1,0:T(8,128)S(1)}, u32[]{:S(2)}, u32[]{:S(2)}) collective-permute-start(f32[8,128]{1,0:T(8,128)S(1)} %get-tuple-element.32.part0_ref), channel_id=1, source_target_pairs={{0,64},{64,128},{128,192},{192,0},{1,65},{65,129},{129,193},{193,1... | collective-permute-start | bytes 12296 | tf_op jit(solution)/shard_map/ppermute | solution.py:339
  8.1 2.6 %collective-permute-start.1 = (f32[8,128]{1,0:T(8,128)S(1)}, f32[8,128]{1,0:T(8,128)S(1)}, u32[]{:S(2)}, u32[]{:S(2)}) collective-permute-start(f32[8,128]{1,0:T(8,128)S(1)} %get-tuple-element.32.part0_ref), channel_id=1, source_target_pairs={{0,128},{64,192},{128,0},{192,64},{1,129},{65,193},{129,1},{193,65... | collective-permute-start | bytes 12296 | tf_op jit(solution)/shard_map/ppermute | solution.py:339
  10.7 1.1 collective-permute-start.2
  12.0 1.4 %collective-permute-done.2.part3_ref = f32[8,128]{1,0:T(8,128)S(1)} collective-permute-done((f32[8,128]{1,0:T(8,128)S(1)}, f32[8,128]{1,0:T(8,128)S(1)}, u32[]{:S(2)}, u32[]{:S(2)}) %collective-permute-start.2) | collective-permute-done | bytes 4128 | tf_op jit(solution)/shard_map/ppermute | solution.py:339
  14.3 20.2 %all_to_all.20.own_ref = bf16[32,24,128]{2,1,0:T(8,128)(2,1)S(1)} all-to-all(bf16[32,24,128]{2,1,0:T(8,128)(2,1)S(1)} %get-tuple-element.34), channel_id=1, replica_groups=mesh['rows'=4,'x'=4,'z'=8,'core'=2] {'x','z'}, dimensions={0} | all-to-all | bytes 393216 | tf_op jit(solution)/shard_map/all_to_all | solution.py:345
  34.5 3.8 %collective-permute-start.3 = (bf16[32,24,128]{2,1,0:T(8,128)(2,1)S(1)}, bf16[32,24,128]{2,1,0:T(8,128)(2,1)S(1)}, u32[]{:S(2)}, u32[]{:S(2)}) collective-permute-start(bf16[32,24,128]{2,1,0:T(8,128)(2,1)S(1)} %all_to_all.20.own_ref), channel_id=1, source_target_pairs={{0,1},{1,0},{2,3},{3,2},{4,5},{5,4},{6,7},{7,6},{8,9},{9,8},{10,11... | collective-permute-start | bytes 589832 | tf_op jit(solution)/shard_map/ppermute | solution.py:346
  38.3 1.1 collective-permute-done.3.other_ref
  39.4 1.3 %shard_map.97 = (f32[16,128]{1,0:T(8,128)S(1)}, f32[32,128]{1,0:T(8,128)S(1)}, f32[256,256]{1,0:T(8,128)S(1)}, f32[8,256]{1,0:T(8,128)S(1)}, f32[256,256]{1,0:T(8,128)S(1)}) custom-call(f32[8,512]{1,0:T(8,128)S(1)} %get-tuple-element.29.masks_ref, bf16[16,256]{1,0:T(8,128)(2,1)S(1)} %get-tuple-element.30.pick_ref, bf16[4,512,512]{2,1,0:T(8,128)(2,1)S(1)} %bitcast.11, ...), custom_call_target="tpu_custom_call" | custom-call | tf_op jit(solution)/shard_map/pallas_call | solution.py:353
  40.8 3.4 %collective-permute-start.5 = (f32[16,128]{1,0:T(8,128)S(1)}, f32[16,128]{1,0:T(8,128)S(1)}, u32[]{:S(2)}, u32[]{:S(2)}) collective-permute-start(f32[16,128]{1,0:T(8,128)S(1)} %get-tuple-element.37.part0_ref), channel_id=1, source_target_pairs={{0,128},{64,192},{128,0},{192,64},{1,129},{65,193},{129,1},{193,65... | collective-permute-start | bytes 24584 | tf_op jit(solution)/shard_map/ppermute | solution.py:339
  45.3 1.4 %collective-permute-done.6.part3_ref = f32[16,128]{1,0:T(8,128)S(1)} collective-permute-done((f32[16,128]{1,0:T(8,128)S(1)}, f32[16,128]{1,0:T(8,128)S(1)}, u32[]{:S(2)}, u32[]{:S(2)}) %collective-permute-start.6) | collective-permute-done | bytes 8224 | tf_op jit(solution)/shard_map/ppermute | solution.py:339
  47.6 13.0 %all_to_all.21.own_ref = bf16[32,24,128]{2,1,0:T(8,128)(2,1)S(1)} all-to-all(bf16[32,24,128]{2,1,0:T(8,128)(2,1)S(1)} %get-tuple-element.41), channel_id=1, replica_groups=mesh['rows'=4,'x'=4,'z'=8,'core'=2] {'x','z'}, dimensions={0} | all-to-all | bytes 393216 | tf_op jit(solution)/shard_map/all_to_all | solution.py:345
  60.6 3.8 %collective-permute-start.7 = (bf16[32,24,128]{2,1,0:T(8,128)(2,1)S(1)}, bf16[32,24,128]{2,1,0:T(8,128)(2,1)S(1)}, u32[]{:S(2)}, u32[]{:S(2)}) collective-permute-start(bf16[32,24,128]{2,1,0:T(8,128)(2,1)S(1)} %all_to_all.21.own_ref), channel_id=1, source_target_pairs={{0,1},{1,0},{2,3},{3,2},{4,5},{5,4},{6,7},{7,6},{8,9},{9,8},{10,11... | collective-permute-start | bytes 589832 | tf_op jit(solution)/shard_map/ppermute | solution.py:346
  64.4 1.1 collective-permute-done.7.other_ref
  65.4 1.0 shard_map.99
  66.4 1.2 %collective-permute-start.10 = (f32[16,128]{1,0:T(8,128)S(1)}, f32[16,128]{1,0:T(8,128)S(1)}, u32[]{:S(2)}, u32[]{:S(2)}) collective-permute-start(f32[16,128]{1,0:T(8,128)S(1)} %get-tuple-element.43.part0_ref), channel_id=1, source_target_pairs={{0,192},{64,0},{128,64},{192,128},{1,193},{65,1},{129,65},{193,129... | collective-permute-start | bytes 24584 | tf_op jit(solution)/shard_map/ppermute | solution.py:339
  67.9 1.2 collective-permute-start.9
  69.1 2.2 %collective-permute-done.8.part1_ref = f32[16,128]{1,0:T(8,128)S(1)} collective-permute-done((f32[16,128]{1,0:T(8,128)S(1)}, f32[16,128]{1,0:T(8,128)S(1)}, u32[]{:S(2)}, u32[]{:S(2)}) %collective-permute-start.8) | collective-permute-done | bytes 8224 | tf_op jit(solution)/shard_map/ppermute | solution.py:339
  72.9 12.9 %all_to_all.22.own_ref = bf16[32,24,128]{2,1,0:T(8,128)(2,1)S(1)} all-to-all(bf16[32,24,128]{2,1,0:T(8,128)(2,1)S(1)} %get-tuple-element.46), channel_id=1, replica_groups=mesh['rows'=4,'x'=4,'z'=8,'core'=2] {'x','z'}, dimensions={0} | all-to-all | bytes 393216 | tf_op jit(solution)/shard_map/all_to_all | solution.py:345
  85.7 3.8 %collective-permute-start.11 = (bf16[32,24,128]{2,1,0:T(8,128)(2,1)S(1)}, bf16[32,24,128]{2,1,0:T(8,128)(2,1)S(1)}, u32[]{:S(2)}, u32[]{:S(2)}) collective-permute-start(bf16[32,24,128]{2,1,0:T(8,128)(2,1)S(1)} %all_to_all.22.own_ref), channel_id=1, source_target_pairs={{0,1},{1,0},{2,3},{3,2},{4,5},{5,4},{6,7},{7,6},{8,9},{9,8},{10,11... | collective-permute-start | bytes 589832 | tf_op jit(solution)/shard_map/ppermute | solution.py:346
  89.5 1.1 collective-permute-done.11.other_ref
  90.6 1.0 shard_map.101
  91.6 3.4 %collective-permute-start.13 = (f32[16,128]{1,0:T(8,128)S(1)}, f32[16,128]{1,0:T(8,128)S(1)}, u32[]{:S(2)}, u32[]{:S(2)}) collective-permute-start(f32[16,128]{1,0:T(8,128)S(1)} %get-tuple-element.48.part0_ref), channel_id=1, source_target_pairs={{0,128},{64,192},{128,0},{192,64},{1,129},{65,193},{129,1},{193,65... | collective-permute-start | bytes 24584 | tf_op jit(solution)/shard_map/ppermute | solution.py:339
  96.2 1.3 %collective-permute-done.14.part3_ref = f32[16,128]{1,0:T(8,128)S(1)} collective-permute-done((f32[16,128]{1,0:T(8,128)S(1)}, f32[16,128]{1,0:T(8,128)S(1)}, u32[]{:S(2)}, u32[]{:S(2)}) %collective-permute-start.14) | collective-permute-done | bytes 8224 | tf_op jit(solution)/shard_map/ppermute | solution.py:339
  97.5 0.9 shard_map.102
  98.5 12.9 %all_to_all.23.own_ref = bf16[32,24,128]{2,1,0:T(8,128)(2,1)S(1)} all-to-all(bf16[32,24,128]{2,1,0:T(8,128)(2,1)S(1)} %get-tuple-element.51), channel_id=1, replica_groups=mesh['rows'=4,'x'=4,'z'=8,'core'=2] {'x','z'}, dimensions={0} | all-to-all | bytes 393216 | tf_op jit(solution)/shard_map/all_to_all | solution.py:345
  111.3 3.8 %collective-permute-start.15 = (bf16[32,24,128]{2,1,0:T(8,128)(2,1)S(1)}, bf16[32,24,128]{2,1,0:T(8,128)(2,1)S(1)}, u32[]{:S(2)}, u32[]{:S(2)}) collective-permute-start(bf16[32,24,128]{2,1,0:T(8,128)(2,1)S(1)} %all_to_all.23.own_ref), channel_id=1, source_target_pairs={{0,1},{1,0},{2,3},{3,2},{4,5},{5,4},{6,7},{7,6},{8,9},{9,8},{10,11... | collective-permute-start | bytes 589832 | tf_op jit(solution)/shard_map/ppermute | solution.py:346
  115.1 1.1 collective-permute-done.15.other_ref
  116.6 2.4 %collective-permute-start.17 = (f32[8,128]{1,0:T(8,128)S(1)}, f32[8,128]{1,0:T(8,128)S(1)}, u32[]{:S(2)}, u32[]{:S(2)}) collective-permute-start(f32[8,128]{1,0:T(8,128)S(1)} %get-tuple-element.53.part0_ref), channel_id=1, source_target_pairs={{0,128},{64,192},{128,0},{192,64},{1,129},{65,193},{129,1},{193,65... | collective-permute-start | bytes 12296 | tf_op jit(solution)/shard_map/ppermute | solution.py:339
  120.6 1.1 collective-permute-done.18.part3_ref
  (37 shorter events, 10.5 us)
Async XLA Ops:
  0.7 12.8 %copy-start.3 = (f32[1024]{0:T(1024)S(1)}, f32[1024]{0:T(1024)}, u32[]{:S(2)}) copy-start(f32[1024]{0:T(1024)} %param.14) | copy-start | bytes 12292
  0.7 12.7 %copy-start.4 = (f32[1024]{0:T(1024)S(1)}, f32[1024]{0:T(1024)}, u32[]{:S(2)}) copy-start(f32[1024]{0:T(1024)} %param.15) | copy-start | bytes 12292
  3.1 1.6 %copy-start = (bf16[1,4,512,512]{3,2,1,0:T(8,128)(2,1)S(1)}, bf16[1,4,512,512]{3,2,1,0:T(8,128)(2,1)}, u32[]{:S(2)}) copy-start(bf16[1,4,512,512]{3,2,1,0:T(8,128)(2,1)} %param.8) | copy-start | bytes 6291460
  4.7 8.7 %copy-start.1 = (bf16[1,4,512,512]{3,2,1,0:T(8,128)(2,1)S(1)}, bf16[1,4,512,512]{3,2,1,0:T(8,128)(2,1)}, u32[]{:S(2)}) copy-start(bf16[1,4,512,512]{3,2,1,0:T(8,128)(2,1)} %param.8) | copy-start | bytes 6291460
  5.8 33.6 %copy-start.2 = (f32[65536]{0:T(1024)S(1)}, f32[65536]{0:T(1024)}, u32[]{:S(2)}) copy-start(f32[65536]{0:T(1024)} %param.13) | copy-start | bytes 786436
  5.9 5.9 %collective-permute-start = (f32[8,128]{1,0:T(8,128)S(1)}, f32[8,128]{1,0:T(8,128)S(1)}, u32[]{:S(2)}, u32[]{:S(2)}) collective-permute-start(f32[8,128]{1,0:T(8,128)S(1)} %get-tuple-element.32.part0_ref), channel_id=1, source_target_pairs={{0,64},{64,128},{128,192},{192,0},{1,65},{65,129},{129,193},{193,1... | collective-permute-start | bytes 12296 | tf_op jit(solution)/shard_map/ppermute | solution.py:339
  8.1 4.0 %collective-permute-start.1 = (f32[8,128]{1,0:T(8,128)S(1)}, f32[8,128]{1,0:T(8,128)S(1)}, u32[]{:S(2)}, u32[]{:S(2)}) collective-permute-start(f32[8,128]{1,0:T(8,128)S(1)} %get-tuple-element.32.part0_ref), channel_id=1, source_target_pairs={{0,128},{64,192},{128,0},{192,64},{1,129},{65,193},{129,1},{193,65... | collective-permute-start | bytes 12296 | tf_op jit(solution)/shard_map/ppermute | solution.py:339
  10.7 2.8 %collective-permute-start.2 = (f32[8,128]{1,0:T(8,128)S(1)}, f32[8,128]{1,0:T(8,128)S(1)}, u32[]{:S(2)}, u32[]{:S(2)}) collective-permute-start(f32[8,128]{1,0:T(8,128)S(1)} %get-tuple-element.32.part0_ref), channel_id=1, source_target_pairs={{0,192},{64,0},{128,64},{192,128},{1,193},{65,1},{129,65},{193,129... | collective-permute-start | bytes 12296 | tf_op jit(solution)/shard_map/ppermute | solution.py:339
  34.5 4.9 %collective-permute-start.3 = (bf16[32,24,128]{2,1,0:T(8,128)(2,1)S(1)}, bf16[32,24,128]{2,1,0:T(8,128)(2,1)S(1)}, u32[]{:S(2)}, u32[]{:S(2)}) collective-permute-start(bf16[32,24,128]{2,1,0:T(8,128)(2,1)S(1)} %all_to_all.20.own_ref), channel_id=1, source_target_pairs={{0,1},{1,0},{2,3},{3,2},{4,5},{5,4},{6,7},{7,6},{8,9},{9,8},{10,11... | collective-permute-start | bytes 589832 | tf_op jit(solution)/shard_map/ppermute | solution.py:346
  40.7 3.8 %collective-permute-start.4 = (f32[16,128]{1,0:T(8,128)S(1)}, f32[16,128]{1,0:T(8,128)S(1)}, u32[]{:S(2)}, u32[]{:S(2)}) collective-permute-start(f32[16,128]{1,0:T(8,128)S(1)} %get-tuple-element.37.part0_ref), channel_id=1, source_target_pairs={{0,64},{64,128},{128,192},{192,0},{1,65},{65,129},{129,193},{193,1... | collective-permute-start | bytes 24584 | tf_op jit(solution)/shard_map/ppermute | solution.py:339
  40.8 4.5 %collective-permute-start.5 = (f32[16,128]{1,0:T(8,128)S(1)}, f32[16,128]{1,0:T(8,128)S(1)}, u32[]{:S(2)}, u32[]{:S(2)}) collective-permute-start(f32[16,128]{1,0:T(8,128)S(1)} %get-tuple-element.37.part0_ref), channel_id=1, source_target_pairs={{0,128},{64,192},{128,0},{192,64},{1,129},{65,193},{129,1},{193,65... | collective-permute-start | bytes 24584 | tf_op jit(solution)/shard_map/ppermute | solution.py:339
  44.2 2.5 %collective-permute-start.6 = (f32[16,128]{1,0:T(8,128)S(1)}, f32[16,128]{1,0:T(8,128)S(1)}, u32[]{:S(2)}, u32[]{:S(2)}) collective-permute-start(f32[16,128]{1,0:T(8,128)S(1)} %get-tuple-element.37.part0_ref), channel_id=1, source_target_pairs={{0,192},{64,0},{128,64},{192,128},{1,193},{65,1},{129,65},{193,129... | collective-permute-start | bytes 24584 | tf_op jit(solution)/shard_map/ppermute | solution.py:339
  60.6 4.8 %collective-permute-start.7 = (bf16[32,24,128]{2,1,0:T(8,128)(2,1)S(1)}, bf16[32,24,128]{2,1,0:T(8,128)(2,1)S(1)}, u32[]{:S(2)}, u32[]{:S(2)}) collective-permute-start(bf16[32,24,128]{2,1,0:T(8,128)(2,1)S(1)} %all_to_all.21.own_ref), channel_id=1, source_target_pairs={{0,1},{1,0},{2,3},{3,2},{4,5},{5,4},{6,7},{7,6},{8,9},{9,8},{10,11... | collective-permute-start | bytes 589832 | tf_op jit(solution)/shard_map/ppermute | solution.py:346
  66.4 2.7 %collective-permute-start.10 = (f32[16,128]{1,0:T(8,128)S(1)}, f32[16,128]{1,0:T(8,128)S(1)}, u32[]{:S(2)}, u32[]{:S(2)}) collective-permute-start(f32[16,128]{1,0:T(8,128)S(1)} %get-tuple-element.43.part0_ref), channel_id=1, source_target_pairs={{0,192},{64,0},{128,64},{192,128},{1,193},{65,1},{129,65},{193,129... | collective-permute-start | bytes 24584 | tf_op jit(solution)/shard_map/ppermute | solution.py:339
  67.6 3.7 %collective-permute-start.8 = (f32[16,128]{1,0:T(8,128)S(1)}, f32[16,128]{1,0:T(8,128)S(1)}, u32[]{:S(2)}, u32[]{:S(2)}) collective-permute-start(f32[16,128]{1,0:T(8,128)S(1)} %get-tuple-element.43.part0_ref), channel_id=1, source_target_pairs={{0,64},{64,128},{128,192},{192,0},{1,65},{65,129},{129,193},{193,1... | collective-permute-start | bytes 24584 | tf_op jit(solution)/shard_map/ppermute | solution.py:339
  67.9 4.0 %collective-permute-start.9 = (f32[16,128]{1,0:T(8,128)S(1)}, f32[16,128]{1,0:T(8,128)S(1)}, u32[]{:S(2)}, u32[]{:S(2)}) collective-permute-start(f32[16,128]{1,0:T(8,128)S(1)} %get-tuple-element.43.part0_ref), channel_id=1, source_target_pairs={{0,128},{64,192},{128,0},{192,64},{1,129},{65,193},{129,1},{193,65... | collective-permute-start | bytes 24584 | tf_op jit(solution)/shard_map/ppermute | solution.py:339
  85.7 4.8 %collective-permute-start.11 = (bf16[32,24,128]{2,1,0:T(8,128)(2,1)S(1)}, bf16[32,24,128]{2,1,0:T(8,128)(2,1)S(1)}, u32[]{:S(2)}, u32[]{:S(2)}) collective-permute-start(bf16[32,24,128]{2,1,0:T(8,128)(2,1)S(1)} %all_to_all.22.own_ref), channel_id=1, source_target_pairs={{0,1},{1,0},{2,3},{3,2},{4,5},{5,4},{6,7},{7,6},{8,9},{9,8},{10,11... | collective-permute-start | bytes 589832 | tf_op jit(solution)/shard_map/ppermute | solution.py:346
  91.5 3.8 %collective-permute-start.12 = (f32[16,128]{1,0:T(8,128)S(1)}, f32[16,128]{1,0:T(8,128)S(1)}, u32[]{:S(2)}, u32[]{:S(2)}) collective-permute-start(f32[16,128]{1,0:T(8,128)S(1)} %get-tuple-element.48.part0_ref), channel_id=1, source_target_pairs={{0,64},{64,128},{128,192},{192,0},{1,65},{65,129},{129,193},{193,1... | collective-permute-start | bytes 24584 | tf_op jit(solution)/shard_map/ppermute | solution.py:339
  91.6 4.6 %collective-permute-start.13 = (f32[16,128]{1,0:T(8,128)S(1)}, f32[16,128]{1,0:T(8,128)S(1)}, u32[]{:S(2)}, u32[]{:S(2)}) collective-permute-start(f32[16,128]{1,0:T(8,128)S(1)} %get-tuple-element.48.part0_ref), channel_id=1, source_target_pairs={{0,128},{64,192},{128,0},{192,64},{1,129},{65,193},{129,1},{193,65... | collective-permute-start | bytes 24584 | tf_op jit(solution)/shard_map/ppermute | solution.py:339
  95.0 2.5 %collective-permute-start.14 = (f32[16,128]{1,0:T(8,128)S(1)}, f32[16,128]{1,0:T(8,128)S(1)}, u32[]{:S(2)}, u32[]{:S(2)}) collective-permute-start(f32[16,128]{1,0:T(8,128)S(1)} %get-tuple-element.48.part0_ref), channel_id=1, source_target_pairs={{0,192},{64,0},{128,64},{192,128},{1,193},{65,1},{129,65},{193,129... | collective-permute-start | bytes 24584 | tf_op jit(solution)/shard_map/ppermute | solution.py:339
  111.3 4.8 %collective-permute-start.15 = (bf16[32,24,128]{2,1,0:T(8,128)(2,1)S(1)}, bf16[32,24,128]{2,1,0:T(8,128)(2,1)S(1)}, u32[]{:S(2)}, u32[]{:S(2)}) collective-permute-start(bf16[32,24,128]{2,1,0:T(8,128)(2,1)S(1)} %all_to_all.23.own_ref), channel_id=1, source_target_pairs={{0,1},{1,0},{2,3},{3,2},{4,5},{5,4},{6,7},{7,6},{8,9},{9,8},{10,11... | collective-permute-start | bytes 589832 | tf_op jit(solution)/shard_map/ppermute | solution.py:346
  116.5 4.1 %collective-permute-start.16 = (f32[8,128]{1,0:T(8,128)S(1)}, f32[8,128]{1,0:T(8,128)S(1)}, u32[]{:S(2)}, u32[]{:S(2)}) collective-permute-start(f32[8,128]{1,0:T(8,128)S(1)} %get-tuple-element.53.part0_ref), channel_id=1, source_target_pairs={{0,64},{64,128},{128,192},{192,0},{1,65},{65,129},{129,193},{193,1... | collective-permute-start | bytes 12296 | tf_op jit(solution)/shard_map/ppermute | solution.py:339
  116.6 4.0 %collective-permute-start.17 = (f32[8,128]{1,0:T(8,128)S(1)}, f32[8,128]{1,0:T(8,128)S(1)}, u32[]{:S(2)}, u32[]{:S(2)}) collective-permute-start(f32[8,128]{1,0:T(8,128)S(1)} %get-tuple-element.53.part0_ref), channel_id=1, source_target_pairs={{0,128},{64,192},{128,0},{192,64},{1,129},{65,193},{129,1},{193,65... | collective-permute-start | bytes 12296 | tf_op jit(solution)/shard_map/ppermute | solution.py:339
  118.9 2.8 %collective-permute-start.18 = (f32[8,128]{1,0:T(8,128)S(1)}, f32[8,128]{1,0:T(8,128)S(1)}, u32[]{:S(2)}, u32[]{:S(2)}) collective-permute-start(f32[8,128]{1,0:T(8,128)S(1)} %get-tuple-element.53.part0_ref), channel_id=1, source_target_pairs={{0,192},{64,0},{128,64},{192,128},{1,193},{65,1},{129,65},{193,129... | collective-permute-start | bytes 12296 | tf_op jit(solution)/shard_map/ppermute | solution.py:339

commit v2 on v1

v2 whole, which is shorter than its diff:
```python
import functools
import math

import jax
import jax.numpy as jnp
from jax import lax
from jax.experimental import pallas as pl
from jax.experimental.pallas import tpu as pltpu
from jax.sharding import Mesh, PartitionSpec as P

ITERS = 4
LANES = 128
SLOTS = 4
TILE = 512
CHUNKS = TILE // LANES
PRODUCT_ROWS = SLOTS * CHUNKS
MESSAGE_ROWS = PRODUCT_ROWS + 8
FINE = (0, 1, 2, 3)

damping = 1.0

NN = (((1,), (0,)), ((), ()))
NT = (((1,), (1,)), ((), ()))


def haar_signs(size):
    row = lax.broadcasted_iota(jnp.int32, (size, size), 0)
    column = lax.broadcasted_iota(jnp.int32, (size, size), 1)
    level = haar_levels(row, size)
    shift = size.bit_length() - 1 - level
    place = column - jnp.left_shift(row - jnp.left_shift(1, level), shift)
    support = jnp.left_shift(1, shift)
    signs = jnp.where(place < jnp.right_shift(support, 1), 1.0, -1.0)
    signs = jnp.where((place >= 0) & (place < support), signs, 0.0)
    return jnp.where(row == 0, 1.0, signs).astype(jnp.bfloat16)


def haar_levels(row, size):
    level = jnp.zeros_like(row)
    for bit in range(1, size.bit_length() - 1):
        level = level + (row >= 1 << bit).astype(jnp.int32)
    return level


def haar_scales(size):
    row = lax.broadcasted_iota(jnp.int32, (1, size), 1)
    scales = jnp.full((1, size), 1.0 / math.sqrt(size), jnp.float32)
    for bit in range(1, size.bit_length() - 1):
        scales = jnp.where(row >= 1 << bit, math.sqrt((1 << bit) / size), scales)
    return scales


def matmul(a, b, dims):
    return lax.dot_general(a, b, dims, preferred_element_type=jnp.float32)


def split3(value):
    high = value.astype(jnp.bfloat16).astype(jnp.float32)
    rest = value - high
    middle = rest.astype(jnp.bfloat16).astype(jnp.float32)
    low = (rest - middle).astype(jnp.bfloat16).astype(jnp.float32)
    return high, middle, low


def total(values):
    return jnp.sum(jnp.sum(values, axis=0, keepdims=True), axis=1, keepdims=True)


def to_rows(values):
    return jnp.concatenate(
        [
            values[b : b + 1, LANES * k : LANES * (k + 1)]
            for b in range(values.shape[0])
            for k in range(CHUNKS)
        ],
        axis=0,
    )


def lane_parts(values):
    parts = sum(values[:, LANES * k : LANES * (k + 1)] for k in range(1, CHUNKS))
    return jnp.sum(values[:, :LANES] + parts, axis=0, keepdims=True)


def times_haar(vectors, signs_ref, dims):
    parts = jnp.concatenate(split3(vectors) + (jnp.zeros((10, TILE), jnp.float32),), axis=0)
    product = matmul(parts.astype(jnp.bfloat16), signs_ref[...], dims)
    return product[0:2] + product[2:4] + product[4:6]


def slot_products(vectors, tiles_ref, dims):
    vectors = jnp.concatenate([vectors, jnp.zeros((12, TILE), jnp.float32)], axis=0)
    vectors = vectors.astype(jnp.bfloat16)
    row = lax.broadcasted_iota(jnp.int32, (SLOTS, TILE), 0)
    out = jnp.zeros((SLOTS, TILE), jnp.float32)
    for s in range(SLOTS):
        out = jnp.where(row == s, matmul(vectors, tiles_ref[s], dims)[0:SLOTS], out)
    return out


def adjoint_sums(picked, masks_ref, tiles_ref):
    products = slot_products(picked, tiles_ref, NN)
    sums = [
        jnp.sum(masks_ref[SLOTS * m : SLOTS * (m + 1), :] * products, axis=0, keepdims=True)
        for m in range(2)
    ]
    return jnp.concatenate(sums, axis=0)


def summed_cells(sums, signs_ref):
    return times_haar(sums * haar_scales(TILE), signs_ref, NN)


def forward_message(cells, residual, direction, masks_ref, ids_ref, tiles_ref, analysis_ref,
                    message_ref, dims):
    coeffs = times_haar(cells, analysis_ref, dims) * haar_scales(TILE)
    picked = masks_ref[0:SLOTS, :] * coeffs[0:1] + masks_ref[SLOTS : 2 * SLOTS, :] * coeffs[1:2]
    products = slot_products(picked, tiles_ref, dims)
    norm = split3(lane_parts(residual * residual))
    cross = split3(lane_parts(residual * direction))
    high, low, _ = split3(products)
    sent = (high, low) if message_ref.shape[1] > MESSAGE_ROWS else (high,)
    pieces = [part[:, LANES * k : LANES * (k + 1)] for part in sent for k in range(CHUNKS)]
    pieces += list(norm) + list(cross) + [ids_ref[0:2, :]]
    message = jnp.concatenate(pieces, axis=0).astype(jnp.bfloat16)
    message_ref[...] = jnp.broadcast_to(message[None], message_ref.shape)


def my_plane():
    return lax.axis_index("x") * lax.axis_size("z") + lax.axis_index("z")


def my_column():
    return my_plane() * lax.axis_size("core") + lax.axis_index("core")


def turn_kernel(tiles_ref, signs_ref, turned_ref, analysis_ref):
    for s in range(SLOTS):
        turned_ref[s] = tiles_ref[s].T
    analysis_ref[...] = signs_ref[...].T


def prepare_kernel(slots_ref, weight_ref, masks_ref, ids_ref, pick_ref, squared_ref):
    rows = [slots_ref[0, s] for s in range(SLOTS)]
    column = lax.broadcasted_iota(jnp.int32, (1, TILE), 1)
    masks_ref[...] = jnp.concatenate(
        [
            (
                column < jnp.where(slots_ref[0, SLOTS + s] == m, slots_ref[0, 2 * SLOTS + s], 0)
            ).astype(jnp.float32)
            for m in range(2)
            for s in range(SLOTS)
        ],
        axis=0,
    )
    lane = lax.broadcasted_iota(jnp.int32, (8, LANES), 1)
    plane = lax.broadcasted_iota(jnp.int32, (8, LANES), 0) * (LANES // 8) + lane // 8
    row_ids = jnp.zeros((8, LANES), jnp.int32)
    for u in range(2 * SLOTS):
        row_ids = jnp.where(lane % 8 == u, rows[u % SLOTS] + (u // SLOTS) * LANES, row_ids)
    ids_ref[...] = jnp.where(plane == my_plane(), row_ids, 0).astype(jnp.float32)
    wide = lax.broadcasted_iota(jnp.int32, (1, 2 * LANES), 1)
    picks = [(wide == row + p * LANES).astype(jnp.float32) for p in range(2) for row in rows]
    pick_ref[...] = jnp.concatenate(
        picks + [jnp.zeros((8, 2 * LANES), jnp.float32)], axis=0
    ).astype(jnp.bfloat16)
    for p in range(2):
        for j in range(2):
            weight = weight_ref[pl.ds(2 * j + p, LANES, stride=CHUNKS), :]
            squared_ref[LANES * p : LANES * (p + 1), LANES * j : LANES * (j + 1)] = weight * weight


def first_forward_kernel(masks_ref, ids_ref, tiles_ref, signs_ref, depth_ref, density_ref, part0_ref,
                         part1_ref, part2_ref, part3_ref, message_ref, residual_ref):
    sums = (part0_ref[...] + part2_ref[...]) + (part1_ref[...] + part3_ref[...])
    residual = depth_ref[...] * summed_cells(sums, signs_ref) - damping * density_ref[...]
    residual_ref[...] = residual
    forward_message(depth_ref[...] * residual, residual, jnp.zeros_like(residual), masks_ref, ids_ref,
                    tiles_ref, signs_ref, message_ref, NT)


def gathered(ref):
    values = ref[...].astype(jnp.float32)
    wide = ref.shape[0] * 8
    last = ref.shape[1] - 8
    halves = [
        jnp.concatenate(
            [values[:, n + 8 * j : n + 8 * j + 8, :].reshape(wide, LANES) for j in range(2)], axis=1
        ).astype(jnp.bfloat16)
        for n in range(0, last, PRODUCT_ROWS)
    ]
    return halves, jnp.sum(values[:, last:, :], axis=0)


def summed_field(ids, halves):
    wide = halves[0][0].shape[0]
    index = lax.broadcasted_iota(jnp.int32, (2 * LANES, wide), 0).astype(jnp.float32)
    fields = []
    for row, parts in zip(ids, halves):
        place = (index == row).astype(jnp.bfloat16)
        fields.append(sum(matmul(place, part, NN) for part in parts[::-1]))
    return fields[0] + fields[1]


def write_scalars(scalars_ref, share_ref, norm_now, direction_norm, field_ref):
    scalars_ref[0:8, :] = jnp.broadcast_to(norm_now, (8, LANES))
    scalars_ref[8:16, :] = jnp.broadcast_to(direction_norm, (8, LANES))
    column = my_column()
    share = []
    for b in range(2):
        rows = [field_ref[pl.ds(p * LANES + 2 * column + b, 1), :] for p in range(2)]
        share += [rows[k % 2][:, LANES * (k // 2) : LANES * (k // 2 + 1)] for k in range(CHUNKS)]
    share_ref[...] = jnp.concatenate(share, axis=0)


def weigh(squared, field):
    weighted = (squared * field).astype(jnp.bfloat16)
    norm = jnp.sum(
        (weighted.astype(jnp.float32) * field).reshape(2 * LANES // 8, 8, 2 * LANES), axis=0
    )
    norm = norm[:, :LANES] + norm[:, LANES:]
    return weighted, (norm[0:2] + norm[2:4]) + (norm[4:6] + norm[6:8])


def slot_blocks(pick_ref, weighted):
    picked = matmul(pick_ref[...], weighted, NN)
    return jnp.concatenate(
        [
            picked[SLOTS * (k % 2) : SLOTS * (k % 2 + 1), LANES * (k // 2) : LANES * (k // 2 + 1)]
            for k in range(CHUNKS)
        ],
        axis=1,
    )


def write_parts(part_ref, norm_part, weighted, masks_ref, pick_ref, tiles_ref):
    part_ref[:, 0:TILE] = adjoint_sums(slot_blocks(pick_ref, weighted), masks_ref, tiles_ref)
    part_ref[:, TILE:] = norm_part


def first_data_kernel(masks_ref, pick_ref, tiles_ref, squared_ref, own_ref, other_ref, part_ref,
                      scalars_ref, share_ref, field_ref, ids_ref):
    halves, tails = zip(*(gathered(ref) for ref in (own_ref, other_ref)))
    norm_now = total((tails[0] + tails[1])[0:3])
    ids = [jnp.concatenate([tail[6:7], tail[7:8]], axis=1) for tail in tails]
    for n in range(2):
        ids_ref[n : n + 1, :] = ids[n]
    field = summed_field(ids, halves)
    field_ref[...] = field
    weighted, norm_part = weigh(squared_ref[...], field)
    write_parts(part_ref, norm_part, weighted, masks_ref, pick_ref, tiles_ref)
    write_scalars(scalars_ref, share_ref, norm_now, norm_now, field_ref)


def next_field(residual_ref, direction_in_ref, scalars_in_ref, field_in_ref, ids_ref, own_ref, other_ref):
    halves, tails = zip(*(gathered(ref) for ref in (own_ref, other_ref)))
    sums = tails[0] + tails[1]
    norm_now = total(sums[0:3])
    cross = total(sums[3:6])
    ratio = norm_now / scalars_in_ref[0:1, 0:1]
    field = summed_field([ids_ref[0:1, :], ids_ref[1:2, :]], halves) + ratio * field_in_ref[...]
    direction = residual_ref[...] + ratio * direction_in_ref[...]
    direction_norm = norm_now + ratio * (2.0 * cross + ratio * scalars_in_ref[8:9, 0:1])
    return field, direction, norm_now, direction_norm


def data_kernel(masks_ref, pick_ref, tiles_ref, squared_ref, residual_ref, direction_in_ref,
                scalars_in_ref, field_in_ref, ids_ref, own_ref, other_ref, part_ref, direction_ref,
                scalars_ref, share_ref, field_ref):
    field, direction, norm_now, direction_norm = next_field(
        residual_ref, direction_in_ref, scalars_in_ref, field_in_ref, ids_ref, own_ref, other_ref
    )
    field_ref[...] = field
    direction_ref[...] = direction
    weighted, norm_part = weigh(squared_ref[...], field)
    write_parts(part_ref, norm_part, weighted, masks_ref, pick_ref, tiles_ref)
    write_scalars(scalars_ref, share_ref, norm_now, direction_norm, field_ref)


def last_data_kernel(squared_ref, residual_ref, direction_in_ref, scalars_in_ref, field_in_ref, ids_ref,
                     own_ref, other_ref, part_ref, direction_ref, scalars_ref, share_ref, field_ref):
    field, direction, norm_now, direction_norm = next_field(
        residual_ref, direction_in_ref, scalars_in_ref, field_in_ref, ids_ref, own_ref, other_ref
    )
    field_ref[...] = field
    direction_ref[...] = direction
    part_ref[...] = weigh(squared_ref[...], field)[1]
    write_scalars(scalars_ref, share_ref, norm_now, direction_norm, field_ref)


def step_kernel(started, *refs):
    masks_ref, ids_ref, tiles_ref, signs_ref, analysis_ref, depth_ref = refs[:6]
    residual_in_ref, direction_ref, scalars_ref, share_ref = refs[6:10]
    refs = refs[10:]
    if started:
        solution_in_ref, change_in_ref = refs[:2]
        refs = refs[2:]
    part0_ref, part1_ref, part2_ref, part3_ref = refs[:4]
    message_ref, residual_ref, solution_ref, change_ref = refs[4:]
    sums = (part0_ref[...] + part2_ref[...]) + (part1_ref[...] + part3_ref[...])
    direction = direction_ref[...]
    length = scalars_ref[0:1, 0:1] / (total(sums[:, TILE:]) + damping * scalars_ref[8:9, 0:1])
    image = depth_ref[...] * summed_cells(sums[:, 0:TILE], signs_ref) + damping * direction
    residual = residual_in_ref[...] - length * image
    residual_ref[...] = residual
    solution = length * direction
    change = length * share_ref[...]
    if started:
        solution = solution_in_ref[...] + solution
        change = change_in_ref[...] + change
    solution_ref[...] = solution
    change_ref[...] = change
    forward_message(depth_ref[...] * residual, residual, direction, masks_ref, ids_ref, tiles_ref,
                    analysis_ref, message_ref, NN)


def last_kernel(depth_ref, density_ref, misfit_ref, direction_ref, scalars_ref, share_ref, solution_ref,
                change_ref, part0_ref, part1_ref, part2_ref, part3_ref, density_out_ref,
                misfit_out_ref):
    sums = (part0_ref[...] + part2_ref[...]) + (part1_ref[...] + part3_ref[...])
    length = scalars_ref[0:1, 0:1] / (total(sums) + damping * scalars_ref[8:9, 0:1])
    solution = solution_ref[...] + length * direction_ref[...]
    density_out_ref[...] = to_rows(density_ref[...] + depth_ref[...] * solution)
    misfit_out_ref[...] = misfit_ref[...] - (change_ref[...] + length * share_ref[...])


def shifts_along_rows(values):
    n = lax.axis_size("rows")
    opposite, left, right = (
        lax.ppermute(values, "rows", [(i, (i + step) % n) for i in range(n)]) for step in (2, 1, 3)
    )
    return values, left, opposite, right


def exchange(message):
    own = lax.all_to_all(message, ("x", "z"), 0, 0)
    return own, lax.ppermute(own, "core", [(0, 1), (1, 0)])


def call(kernel, out_shape, operands, scratch=()):
    spaces = [
        pltpu.VMEM if jnp.issubdtype(a.dtype, jnp.floating) else pltpu.SMEM for a in operands
    ]
    return pl.pallas_call(
        kernel,
        out_shape=out_shape,
        in_specs=[pl.BlockSpec(memory_space=space) for space in spaces],
        out_specs=jax.tree.map(lambda _: pl.BlockSpec(memory_space=pltpu.VMEM), out_shape),
        scratch_shapes=list(scratch),
        compiler_params=pltpu.CompilerParams(vmem_limit_bytes=24 * 2**20),
    )(*operands)


def first_sums(tiles, slot_rows, slot_cols, slot_kept, misfit, data_weight):
    weighted = (data_weight * data_weight * misfit).astype(jnp.bfloat16).reshape(-1, TILE)
    blocks = jnp.arange(weighted.shape[0], dtype=jnp.int32)
    picked = jnp.dot(
        (slot_rows[:, None] == blocks[None, :]).astype(jnp.bfloat16),
        weighted,
        preferred_element_type=jnp.float32,
    ).astype(jnp.bfloat16)
    products = jnp.einsum("sab,sa->sb", tiles, picked, preferred_element_type=jnp.float32)
    live = jnp.arange(TILE, dtype=jnp.int32)[None, :] < slot_kept[:, None]
    products = jnp.where(live, products, 0.0)
    pick_cols = slot_cols[None, :] == jnp.arange(2, dtype=jnp.int32)[:, None]
    return jnp.dot(pick_cols.astype(jnp.float32), products, precision=lax.Precision.HIGHEST)


def per_device(
    sensitivity, tile_rows, tile_cols, kept_counts, misfit, data_weight, depth_weight, density
):
    tiles = sensitivity[0]
    signs = haar_signs(TILE)
    turned, analysis = call(
        turn_kernel,
        tuple(jax.ShapeDtypeStruct(a.shape, a.dtype) for a in (tiles, signs)),
        (tiles, signs),
    )
    slots = jnp.concatenate([tile_rows, tile_cols, kept_counts], axis=1)
    depth, density = (a.reshape(2, TILE) for a in (depth_weight, density))
    own_misfit = lax.dynamic_slice_in_dim(misfit.reshape(-1, LANES), my_column() * 8, 8)
    planes = lax.axis_size("x") * lax.axis_size("z")
    f32 = functools.partial(jax.ShapeDtypeStruct, dtype=jnp.float32)
    cells, rows, parts = f32((2, TILE)), f32((8, LANES)), f32((2, TILE + LANES))
    scalars_shape, field_shape = f32((16, LANES)), f32((2 * LANES, 2 * LANES))
    message_shapes = [
        jax.ShapeDtypeStruct(
            (planes, MESSAGE_ROWS + (PRODUCT_ROWS if n in FINE else 0), LANES), jnp.bfloat16
        )
        for n in range(ITERS)
    ]
    pick_shape = jax.ShapeDtypeStruct((16, 2 * LANES), jnp.bfloat16)

    masks, row_ids, pick, squared = call(
        prepare_kernel,
        (f32((8, TILE)), rows, pick_shape, field_shape),
        (slots, data_weight.reshape(-1, LANES)),
    )
    part = first_sums(tiles, tile_rows[0], tile_cols[0], kept_counts[0], misfit, data_weight)
    message, residual = call(
        first_forward_kernel,
        (message_shapes[0], cells),
        (masks, row_ids, tiles, signs, depth, density) + shifts_along_rows(part),
    )
    part, scalars, share, field, ids = call(
        first_data_kernel,
        (parts, scalars_shape, rows, field_shape, f32((8, planes * 8))),
        (masks, pick, tiles, squared) + exchange(message),
    )
    direction = residual
    sofar = ()
    for iteration in range(1, ITERS):
        message, residual, *sofar = call(
            functools.partial(step_kernel, iteration > 1),
            (message_shapes[iteration], cells, cells, rows),
            (masks, row_ids, turned, signs, analysis, depth, residual, direction, scalars, share)
            + (*sofar, *shifts_along_rows(part)),
        )
        carried = (squared, residual, direction, scalars, field, ids) + exchange(message)
        if iteration + 1 < ITERS:
            part, direction, scalars, share, field = call(
                data_kernel,
                (parts, cells, scalars_shape, rows, field_shape),
                (masks, pick, tiles) + carried,
            )
    part, direction, scalars, share = call(
        last_data_kernel,
        (f32((2, LANES)), cells, scalars_shape, rows),
        carried,
        [pltpu.VMEM(field_shape.shape, jnp.float32)],
    )
    new_density, new_misfit = call(
        last_kernel,
        (rows, rows),
        (depth, density, own_misfit, direction, scalars, share, *sofar) + shifts_along_rows(part),
    )
    return (new_density.reshape(-1), new_misfit.reshape(-1))


def solution(mesh):
    cols = ("x", "z", "core")
    fine = Mesh(mesh.devices.reshape(4, 4, 8, 2), ("rows",) + cols)
    return jax.shard_map(
        per_device,
        mesh=fine,
        in_specs=(
            P("rows", cols, None, None),
            P("rows", cols),
            P("rows", cols),
            P("rows", cols),
            P("rows"),
            P("rows"),
            P(cols),
            P(cols),
        ),
        out_specs=(P(cols), P(("rows",) + cols)),
        check_vma=False,
    )
```

time: 123 us -> 130 us (1.057)
  blocking collectives: 58.9 us -> 63.6 us
  starting transfers between devices: 34 us -> 37.8 us
  matrix products: 0 us -> 3.01 us
  waiting for transfers between devices: 14.9 us -> 12.6 us
  local copies, waits for them, and re-layouts: 2.3 us -> 0.83 us
    all_to_all x4, blocking collectives: 58.9 us -> 63.6 us  [exchange(): own = lax.all_to_all(message, ('x', 'z'), 0, 0)]
    dot_general x0 -> x3, matrix products: none -> 3.01 us  [the longest x1 1.96 us: first_sums(): jnp.einsum('sab,sa->sb', tiles, picked, preferred_element_type=jnp.float32)]
    ppermute x15, waiting for transfers between devices: 10.6 us -> 7.62 us  [shifts_along_rows(): lax.ppermute(values, 'rows', [(i, (i + step) % n) for i in range(n)])]
    ppermute x4, starting transfers between devices: 15.1 us -> 17.5 us  [exchange(): return (own, lax.ppermute(own, 'core', [(0, 1), (1, 0)]))]
    unnamed x10 -> x14, local copies, waits for them, and re-layouts: 1.61 us -> 0.03 us
    ppermute x15, starting transfers between devices: 18.9 us -> 20.2 us  [shifts_along_rows(): lax.ppermute(values, 'rows', [(i, (i + step) % n) for i in range(n)])]
    pallas_call x10 -> x11, Pallas kernels: 9.03 us -> 8.81 us  [call(): pl.pallas_call(kernel, out_shape=out_shape, in_specs=[pl.BlockSpec(memory...]
  transfers between devices with their start and end apart: 19 -> 19, of which waited for: 16 -> 12; matrix products, arithmetic and copies ran while one was open for 1% -> 1% of each run, Pallas kernels for 0% -> 1%
where the time goes in v2:
time: 130 us; the launch traced here: 129 us
  blocking collectives  63.6 us (49%)
  starting transfers between devices  37.8 us (29%)
  waiting for transfers between devices  12.6 us (10%)
  Pallas kernels  8.81 us (7%)
  matrix products  3.01 us (2%)
  other arithmetic  1.95 us (2%)
    all_to_all x4, blocking collectives, exchange(): own = lax.all_to_all(message, ('x', 'z'), 0, 0)  63.6 us
    ppermute x15, starting transfers between devices, shifts_along_rows(): lax.ppermute(values, 'rows', [(i, (i + step) % n) for i in range(n)])  20.2 us
    ppermute x4, starting transfers between devices, exchange(): return (own, lax.ppermute(own, 'core', [(0, 1), (1, 0)]))  17.5 us
    pallas_call x11, Pallas kernels, call(): pl.pallas_call(kernel, out_shape=out_shape, in_specs=[pl.BlockSpec(memory...  8.81 us
    ppermute x15, waiting for transfers between devices, shifts_along_rows(): lax.ppermute(values, 'rows', [(i, (i + step) % n) for i in range(n)])  7.62 us
    ppermute x4, waiting for transfers between devices, exchange(): return (own, lax.ppermute(own, 'core', [(0, 1), (1, 0)]))  5.02 us
  transfers between devices with their start and end apart: 19, of which 12 were waited for; matrix products, arithmetic and copies ran while one was open for 1% of the time, Pallas kernels for 1%

profile of v2, /device:TPU:1, one launch (start us, length us, event | category | flops | bytes accessed | tf_op | source)
XLA Modules:
  0.0 129.4 jit_solution(14889065823471792741)
XLA Ops:
  0.7 1.2 multiply_convert_fusion
  2.0 0.8 fusion
  2.9 2.0 %fusion.7 = f32[4,1,512]{2,1,0:T(1,128)S(1)} fusion(bf16[4,512,1]{1,0,2:T(4,128)(2,1)S(1)} %fusion, bf16[1,4,512,512]{3,2,1,0:T(8,128)(2,1)} %param.8), kind=kOutput, calls=%fused_computation.21 | convolution fusion | flops 2097152 | bytes 2109440 | tf_op jit(solution)/shard_map/sab,sa->sb/dot_general | solution.py:362
  5.0 2.1 %collective-permute-start = (f32[2,512]{1,0:T(2,128)S(1)}, f32[2,512]{1,0:T(2,128)S(1)}, u32[]{:S(2)}, u32[]{:S(2)}) collective-permute-start(f32[2,512]{1,0:T(2,128)S(1)} %fusion.5.part0_ref), channel_id=1, source_target_pairs={{0,64},{64,128},{128,192},{192,0},{1,65},{65,129},{129,193},{193,1... | collective-permute-start | bytes 12296 | tf_op jit(solution)/shard_map/ppermute | solution.py:330
  7.2 2.6 %collective-permute-start.1 = (f32[2,512]{1,0:T(2,128)S(1)}, f32[2,512]{1,0:T(2,128)S(1)}, u32[]{:S(2)}, u32[]{:S(2)}) collective-permute-start(f32[2,512]{1,0:T(2,128)S(1)} %fusion.5.part0_ref), channel_id=1, source_target_pairs={{0,128},{64,192},{128,0},{192,64},{1,129},{65,193},{129,1},{193,65... | collective-permute-start | bytes 12296 | tf_op jit(solution)/shard_map/ppermute | solution.py:330
  9.8 1.1 collective-permute-start.2
  12.5 1.0 shard_map.97
  13.6 20.8 %all_to_all.20.own_ref = bf16[32,40,128]{2,1,0:T(8,128)(2,1)S(1)} all-to-all(bf16[32,40,128]{2,1,0:T(8,128)(2,1)S(1)} %get-tuple-element.50), channel_id=1, replica_groups=mesh['rows'=4,'x'=4,'z'=8,'core'=2] {'x','z'}, dimensions={0} | all-to-all | bytes 655360 | tf_op jit(solution)/shard_map/all_to_all | solution.py:336
  34.3 4.4 %collective-permute-start.3 = (bf16[32,40,128]{2,1,0:T(8,128)(2,1)S(1)}, bf16[32,40,128]{2,1,0:T(8,128)(2,1)S(1)}, u32[]{:S(2)}, u32[]{:S(2)}) collective-permute-start(bf16[32,40,128]{2,1,0:T(8,128)(2,1)S(1)} %all_to_all.20.own_ref), channel_id=1, source_target_pairs={{0,1},{1,0},{2,3},{3,2},{4,5},{5,4},{6,7},{7,6},{8,9},{9,8},{10,11... | collective-permute-start | bytes 983048 | tf_op jit(solution)/shard_map/ppermute | solution.py:337
  38.7 1.3 collective-permute-done.3.other_ref
  40.0 1.0 shard_map.98
  41.4 3.3 %collective-permute-start.5 = (f32[2,640]{1,0:T(2,128)S(1)}, f32[2,640]{1,0:T(2,128)S(1)}, u32[]{:S(2)}, u32[]{:S(2)}) collective-permute-start(f32[2,640]{1,0:T(2,128)S(1)} %get-tuple-element.53.refs_10_), channel_id=1, source_target_pairs={{0,128},{64,192},{128,0},{192,64},{1,129},{65,193},{129,1},{193,65... | collective-permute-start | bytes 15368 | tf_op jit(solution)/shard_map/ppermute | solution.py:330
  45.7 1.4 %collective-permute-done.6.refs_13_ = f32[2,640]{1,0:T(2,128)S(1)} collective-permute-done((f32[2,640]{1,0:T(2,128)S(1)}, f32[2,640]{1,0:T(2,128)S(1)}, u32[]{:S(2)}, u32[]{:S(2)}) %collective-permute-start.6) | collective-permute-done | bytes 5152 | tf_op jit(solution)/shard_map/ppermute | solution.py:330
  47.9 13.9 %all_to_all.21.own_ref = bf16[32,40,128]{2,1,0:T(8,128)(2,1)S(1)} all-to-all(bf16[32,40,128]{2,1,0:T(8,128)(2,1)S(1)} %get-tuple-element.57), channel_id=1, replica_groups=mesh['rows'=4,'x'=4,'z'=8,'core'=2] {'x','z'}, dimensions={0} | all-to-all | bytes 655360 | tf_op jit(solution)/shard_map/all_to_all | solution.py:336
  61.9 4.4 %collective-permute-start.7 = (bf16[32,40,128]{2,1,0:T(8,128)(2,1)S(1)}, bf16[32,40,128]{2,1,0:T(8,128)(2,1)S(1)}, u32[]{:S(2)}, u32[]{:S(2)}) collective-permute-start(bf16[32,40,128]{2,1,0:T(8,128)(2,1)S(1)} %all_to_all.21.own_ref), channel_id=1, source_target_pairs={{0,1},{1,0},{2,3},{3,2},{4,5},{5,4},{6,7},{7,6},{8,9},{9,8},{10,11... | collective-permute-start | bytes 983048 | tf_op jit(solution)/shard_map/ppermute | solution.py:337
  66.2 1.3 collective-permute-done.7.other_ref
  67.5 1.0 shard_map.100
  68.5 1.4 %collective-permute-start.10 = (f32[2,640]{1,0:T(2,128)S(1)}, f32[2,640]{1,0:T(2,128)S(1)}, u32[]{:S(2)}, u32[]{:S(2)}) collective-permute-start(f32[2,640]{1,0:T(2,128)S(1)} %get-tuple-element.63.refs_12_), channel_id=1, source_target_pairs={{0,192},{64,0},{128,64},{192,128},{1,193},{65,1},{129,65},{193,129... | collective-permute-start | bytes 15368 | tf_op jit(solution)/shard_map/ppermute | solution.py:330
  70.1 1.6 %collective-permute-start.9 = (f32[2,640]{1,0:T(2,128)S(1)}, f32[2,640]{1,0:T(2,128)S(1)}, u32[]{:S(2)}, u32[]{:S(2)}) collective-permute-start(f32[2,640]{1,0:T(2,128)S(1)} %get-tuple-element.63.refs_12_), channel_id=1, source_target_pairs={{0,128},{64,192},{128,0},{192,64},{1,129},{65,193},{129,1},{193,65... | collective-permute-start | bytes 15368 | tf_op jit(solution)/shard_map/ppermute | solution.py:330
  71.7 1.9 %collective-permute-done.8.refs_13_ = f32[2,640]{1,0:T(2,128)S(1)} collective-permute-done((f32[2,640]{1,0:T(2,128)S(1)}, f32[2,640]{1,0:T(2,128)S(1)}, u32[]{:S(2)}, u32[]{:S(2)}) %collective-permute-start.8) | collective-permute-done | bytes 5152 | tf_op jit(solution)/shard_map/ppermute | solution.py:330
  74.8 14.5 %all_to_all.22.own_ref = bf16[32,40,128]{2,1,0:T(8,128)(2,1)S(1)} all-to-all(bf16[32,40,128]{2,1,0:T(8,128)(2,1)S(1)} %get-tuple-element.66), channel_id=1, replica_groups=mesh['rows'=4,'x'=4,'z'=8,'core'=2] {'x','z'}, dimensions={0} | all-to-all | bytes 655360 | tf_op jit(solution)/shard_map/all_to_all | solution.py:336
  89.4 4.4 %collective-permute-start.11 = (bf16[32,40,128]{2,1,0:T(8,128)(2,1)S(1)}, bf16[32,40,128]{2,1,0:T(8,128)(2,1)S(1)}, u32[]{:S(2)}, u32[]{:S(2)}) collective-permute-start(bf16[32,40,128]{2,1,0:T(8,128)(2,1)S(1)} %all_to_all.22.own_ref), channel_id=1, source_target_pairs={{0,1},{1,0},{2,3},{3,2},{4,5},{5,4},{6,7},{7,6},{8,9},{9,8},{10,11... | collective-permute-start | bytes 983048 | tf_op jit(solution)/shard_map/ppermute | solution.py:337
  93.7 1.3 collective-permute-done.11.other_ref
  95.0 1.1 shard_map.102
  96.5 3.3 %collective-permute-start.13 = (f32[2,640]{1,0:T(2,128)S(1)}, f32[2,640]{1,0:T(2,128)S(1)}, u32[]{:S(2)}, u32[]{:S(2)}) collective-permute-start(f32[2,640]{1,0:T(2,128)S(1)} %get-tuple-element.72.refs_12_), channel_id=1, source_target_pairs={{0,128},{64,192},{128,0},{192,64},{1,129},{65,193},{129,1},{193,65... | collective-permute-start | bytes 15368 | tf_op jit(solution)/shard_map/ppermute | solution.py:330
  99.9 1.1 collective-permute-done.13.refs_14_
  100.9 1.4 %collective-permute-done.14.refs_15_ = f32[2,640]{1,0:T(2,128)S(1)} collective-permute-done((f32[2,640]{1,0:T(2,128)S(1)}, f32[2,640]{1,0:T(2,128)S(1)}, u32[]{:S(2)}, u32[]{:S(2)}) %collective-permute-start.14) | collective-permute-done | bytes 5152 | tf_op jit(solution)/shard_map/ppermute | solution.py:330
  103.1 14.3 %all_to_all.23.own_ref = bf16[32,40,128]{2,1,0:T(8,128)(2,1)S(1)} all-to-all(bf16[32,40,128]{2,1,0:T(8,128)(2,1)S(1)} %get-tuple-element.75), channel_id=1, replica_groups=mesh['rows'=4,'x'=4,'z'=8,'core'=2] {'x','z'}, dimensions={0} | all-to-all | bytes 655360 | tf_op jit(solution)/shard_map/all_to_all | solution.py:336
  117.4 4.4 %collective-permute-start.15 = (bf16[32,40,128]{2,1,0:T(8,128)(2,1)S(1)}, bf16[32,40,128]{2,1,0:T(8,128)(2,1)S(1)}, u32[]{:S(2)}, u32[]{:S(2)}) collective-permute-start(bf16[32,40,128]{2,1,0:T(8,128)(2,1)S(1)} %all_to_all.23.own_ref), channel_id=1, source_target_pairs={{0,1},{1,0},{2,3},{3,2},{4,5},{5,4},{6,7},{7,6},{8,9},{9,8},{10,11... | collective-permute-start | bytes 983048 | tf_op jit(solution)/shard_map/ppermute | solution.py:337
  121.8 1.3 collective-permute-done.15.other_ref
  123.5 2.8 %collective-permute-start.17 = (f32[2,128]{1,0:T(2,128)S(1)}, f32[2,128]{1,0:T(2,128)S(1)}, u32[]{:S(2)}, u32[]{:S(2)}) collective-permute-start(f32[2,128]{1,0:T(2,128)S(1)} %get-tuple-element.81.part0_ref), channel_id=1, source_target_pairs={{0,128},{64,192},{128,0},{192,64},{1,129},{65,193},{129,1},{193,65... | collective-permute-start | bytes 3080 | tf_op jit(solution)/shard_map/ppermute | solution.py:330
  126.3 0.9 collective-permute-start.18
  (48 shorter events, 9.3 us)
Async XLA Ops:
  0.6 11.0 %copy-start.1 = (f32[65536]{0:T(1024)S(1)}, f32[65536]{0:T(1024)}, u32[]{:S(2)}) copy-start(f32[65536]{0:T(1024)} %param.13) | copy-start | bytes 786436
  0.6 10.9 %copy-start.6 = (s32[1,4]{1,0:T(1,128)S(1)}, s32[1,4]{1,0:T(1,128)}, u32[]{:S(2)}) copy-start(s32[1,4]{1,0:T(1,128)} %param.9) | copy-start | bytes 52
  0.7 11.9 %copy-start = (bf16[1,4,512,512]{3,2,1,0:T(8,128)(2,1)S(1)}, bf16[1,4,512,512]{3,2,1,0:T(8,128)(2,1)}, u32[]{:S(2)}) copy-start(bf16[1,4,512,512]{3,2,1,0:T(8,128)(2,1)} %param.8) | copy-start | bytes 6291460
  0.7 4.2 %copy-start.5 = (s32[1,4]{1,0:T(1,128)S(1)}, s32[1,4]{1,0:T(1,128)}, u32[]{:S(2)}) copy-start(s32[1,4]{1,0:T(1,128)} %param.10) | copy-start | bytes 52
  0.7 4.1 %copy-start.4 = (s32[1,4]{1,0:T(1,128)S(1)}, s32[1,4]{1,0:T(1,128)}, u32[]{:S(2)}) copy-start(s32[1,4]{1,0:T(1,128)} %param.11) | copy-start | bytes 52
  0.7 10.9 %copy-start.2 = (f32[1024]{0:T(1024)S(1)}, f32[1024]{0:T(1024)}, u32[]{:S(2)}) copy-start(f32[1024]{0:T(1024)} %param.14) | copy-start | bytes 12292
  0.7 10.9 %copy-start.3 = (f32[1024]{0:T(1024)S(1)}, f32[1024]{0:T(1024)}, u32[]{:S(2)}) copy-start(f32[1024]{0:T(1024)} %param.15) | copy-start | bytes 12292
  5.0 7.2 %collective-permute-start = (f32[2,512]{1,0:T(2,128)S(1)}, f32[2,512]{1,0:T(2,128)S(1)}, u32[]{:S(2)}, u32[]{:S(2)}) collective-permute-start(f32[2,512]{1,0:T(2,128)S(1)} %fusion.5.part0_ref), channel_id=1, source_target_pairs={{0,64},{64,128},{128,192},{192,0},{1,65},{65,129},{129,193},{193,1... | collective-permute-start | bytes 12296 | tf_op jit(solution)/shard_map/ppermute | solution.py:330
  7.2 5.1 %collective-permute-start.1 = (f32[2,512]{1,0:T(2,128)S(1)}, f32[2,512]{1,0:T(2,128)S(1)}, u32[]{:S(2)}, u32[]{:S(2)}) collective-permute-start(f32[2,512]{1,0:T(2,128)S(1)} %fusion.5.part0_ref), channel_id=1, source_target_pairs={{0,128},{64,192},{128,0},{192,64},{1,129},{65,193},{129,1},{193,65... | collective-permute-start | bytes 12296 | tf_op jit(solution)/shard_map/ppermute | solution.py:330
  9.8 2.8 %collective-permute-start.2 = (f32[2,512]{1,0:T(2,128)S(1)}, f32[2,512]{1,0:T(2,128)S(1)}, u32[]{:S(2)}, u32[]{:S(2)}) collective-permute-start(f32[2,512]{1,0:T(2,128)S(1)} %fusion.5.part0_ref), channel_id=1, source_target_pairs={{0,192},{64,0},{128,64},{192,128},{1,193},{65,1},{129,65},{193,129... | collective-permute-start | bytes 12296 | tf_op jit(solution)/shard_map/ppermute | solution.py:330
  34.3 5.6 %collective-permute-start.3 = (bf16[32,40,128]{2,1,0:T(8,128)(2,1)S(1)}, bf16[32,40,128]{2,1,0:T(8,128)(2,1)S(1)}, u32[]{:S(2)}, u32[]{:S(2)}) collective-permute-start(bf16[32,40,128]{2,1,0:T(8,128)(2,1)S(1)} %all_to_all.20.own_ref), channel_id=1, source_target_pairs={{0,1},{1,0},{2,3},{3,2},{4,5},{5,4},{6,7},{7,6},{8,9},{9,8},{10,11... | collective-permute-start | bytes 983048 | tf_op jit(solution)/shard_map/ppermute | solution.py:337
  41.0 4.4 %collective-permute-start.4 = (f32[2,640]{1,0:T(2,128)S(1)}, f32[2,640]{1,0:T(2,128)S(1)}, u32[]{:S(2)}, u32[]{:S(2)}) collective-permute-start(f32[2,640]{1,0:T(2,128)S(1)} %get-tuple-element.53.refs_10_), channel_id=1, source_target_pairs={{0,64},{64,128},{128,192},{192,0},{1,65},{65,129},{129,193},{193,1... | collective-permute-start | bytes 15368 | tf_op jit(solution)/shard_map/ppermute | solution.py:330
  41.4 4.4 %collective-permute-start.5 = (f32[2,640]{1,0:T(2,128)S(1)}, f32[2,640]{1,0:T(2,128)S(1)}, u32[]{:S(2)}, u32[]{:S(2)}) collective-permute-start(f32[2,640]{1,0:T(2,128)S(1)} %get-tuple-element.53.refs_10_), channel_id=1, source_target_pairs={{0,128},{64,192},{128,0},{192,64},{1,129},{65,193},{129,1},{193,65... | collective-permute-start | bytes 15368 | tf_op jit(solution)/shard_map/ppermute | solution.py:330
  44.7 2.5 %collective-permute-start.6 = (f32[2,640]{1,0:T(2,128)S(1)}, f32[2,640]{1,0:T(2,128)S(1)}, u32[]{:S(2)}, u32[]{:S(2)}) collective-permute-start(f32[2,640]{1,0:T(2,128)S(1)} %get-tuple-element.53.refs_10_), channel_id=1, source_target_pairs={{0,192},{64,0},{128,64},{192,128},{1,193},{65,1},{129,65},{193,129... | collective-permute-start | bytes 15368 | tf_op jit(solution)/shard_map/ppermute | solution.py:330
  61.9 5.6 %collective-permute-start.7 = (bf16[32,40,128]{2,1,0:T(8,128)(2,1)S(1)}, bf16[32,40,128]{2,1,0:T(8,128)(2,1)S(1)}, u32[]{:S(2)}, u32[]{:S(2)}) collective-permute-start(bf16[32,40,128]{2,1,0:T(8,128)(2,1)S(1)} %all_to_all.21.own_ref), channel_id=1, source_target_pairs={{0,1},{1,0},{2,3},{3,2},{4,5},{5,4},{6,7},{7,6},{8,9},{9,8},{10,11... | collective-permute-start | bytes 983048 | tf_op jit(solution)/shard_map/ppermute | solution.py:337
  68.5 3.2 %collective-permute-start.10 = (f32[2,640]{1,0:T(2,128)S(1)}, f32[2,640]{1,0:T(2,128)S(1)}, u32[]{:S(2)}, u32[]{:S(2)}) collective-permute-start(f32[2,640]{1,0:T(2,128)S(1)} %get-tuple-element.63.refs_12_), channel_id=1, source_target_pairs={{0,192},{64,0},{128,64},{192,128},{1,193},{65,1},{129,65},{193,129... | collective-permute-start | bytes 15368 | tf_op jit(solution)/shard_map/ppermute | solution.py:330
  70.0 3.7 %collective-permute-start.8 = (f32[2,640]{1,0:T(2,128)S(1)}, f32[2,640]{1,0:T(2,128)S(1)}, u32[]{:S(2)}, u32[]{:S(2)}) collective-permute-start(f32[2,640]{1,0:T(2,128)S(1)} %get-tuple-element.63.refs_12_), channel_id=1, source_target_pairs={{0,64},{64,128},{128,192},{192,0},{1,65},{65,129},{129,193},{193,1... | collective-permute-start | bytes 15368 | tf_op jit(solution)/shard_map/ppermute | solution.py:330
  70.1 4.0 %collective-permute-start.9 = (f32[2,640]{1,0:T(2,128)S(1)}, f32[2,640]{1,0:T(2,128)S(1)}, u32[]{:S(2)}, u32[]{:S(2)}) collective-permute-start(f32[2,640]{1,0:T(2,128)S(1)} %get-tuple-element.63.refs_12_), channel_id=1, source_target_pairs={{0,128},{64,192},{128,0},{192,64},{1,129},{65,193},{129,1},{193,65... | collective-permute-start | bytes 15368 | tf_op jit(solution)/shard_map/ppermute | solution.py:330
  89.4 5.6 %collective-permute-start.11 = (bf16[32,40,128]{2,1,0:T(8,128)(2,1)S(1)}, bf16[32,40,128]{2,1,0:T(8,128)(2,1)S(1)}, u32[]{:S(2)}, u32[]{:S(2)}) collective-permute-start(bf16[32,40,128]{2,1,0:T(8,128)(2,1)S(1)} %all_to_all.22.own_ref), channel_id=1, source_target_pairs={{0,1},{1,0},{2,3},{3,2},{4,5},{5,4},{6,7},{7,6},{8,9},{9,8},{10,11... | collective-permute-start | bytes 983048 | tf_op jit(solution)/shard_map/ppermute | solution.py:337
  96.1 3.8 %collective-permute-start.12 = (f32[2,640]{1,0:T(2,128)S(1)}, f32[2,640]{1,0:T(2,128)S(1)}, u32[]{:S(2)}, u32[]{:S(2)}) collective-permute-start(f32[2,640]{1,0:T(2,128)S(1)} %get-tuple-element.72.refs_12_), channel_id=1, source_target_pairs={{0,64},{64,128},{128,192},{192,0},{1,65},{65,129},{129,193},{193,1... | collective-permute-start | bytes 15368 | tf_op jit(solution)/shard_map/ppermute | solution.py:330
  96.5 4.4 %collective-permute-start.13 = (f32[2,640]{1,0:T(2,128)S(1)}, f32[2,640]{1,0:T(2,128)S(1)}, u32[]{:S(2)}, u32[]{:S(2)}) collective-permute-start(f32[2,640]{1,0:T(2,128)S(1)} %get-tuple-element.72.refs_12_), channel_id=1, source_target_pairs={{0,128},{64,192},{128,0},{192,64},{1,129},{65,193},{129,1},{193,65... | collective-permute-start | bytes 15368 | tf_op jit(solution)/shard_map/ppermute | solution.py:330
  99.9 2.5 %collective-permute-start.14 = (f32[2,640]{1,0:T(2,128)S(1)}, f32[2,640]{1,0:T(2,128)S(1)}, u32[]{:S(2)}, u32[]{:S(2)}) collective-permute-start(f32[2,640]{1,0:T(2,128)S(1)} %get-tuple-element.72.refs_12_), channel_id=1, source_target_pairs={{0,192},{64,0},{128,64},{192,128},{1,193},{65,1},{129,65},{193,129... | collective-permute-start | bytes 15368 | tf_op jit(solution)/shard_map/ppermute | solution.py:330
  117.4 5.6 %collective-permute-start.15 = (bf16[32,40,128]{2,1,0:T(8,128)(2,1)S(1)}, bf16[32,40,128]{2,1,0:T(8,128)(2,1)S(1)}, u32[]{:S(2)}, u32[]{:S(2)}) collective-permute-start(bf16[32,40,128]{2,1,0:T(8,128)(2,1)S(1)} %all_to_all.23.own_ref), channel_id=1, source_target_pairs={{0,1},{1,0},{2,3},{3,2},{4,5},{5,4},{6,7},{7,6},{8,9},{9,8},{10,11... | collective-permute-start | bytes 983048 | tf_op jit(solution)/shard_map/ppermute | solution.py:337
  123.4 4.5 %collective-permute-start.16 = (f32[2,128]{1,0:T(2,128)S(1)}, f32[2,128]{1,0:T(2,128)S(1)}, u32[]{:S(2)}, u32[]{:S(2)}) collective-permute-start(f32[2,128]{1,0:T(2,128)S(1)} %get-tuple-element.81.part0_ref), channel_id=1, source_target_pairs={{0,64},{64,128},{128,192},{192,0},{1,65},{65,129},{129,193},{193,1... | collective-permute-start | bytes 3080 | tf_op jit(solution)/shard_map/ppermute | solution.py:330
  123.5 4.4 %collective-permute-start.17 = (f32[2,128]{1,0:T(2,128)S(1)}, f32[2,128]{1,0:T(2,128)S(1)}, u32[]{:S(2)}, u32[]{:S(2)}) collective-permute-start(f32[2,128]{1,0:T(2,128)S(1)} %get-tuple-element.81.part0_ref), channel_id=1, source_target_pairs={{0,128},{64,192},{128,0},{192,64},{1,129},{65,193},{129,1},{193,65... | collective-permute-start | bytes 3080 | tf_op jit(solution)/shard_map/ppermute | solution.py:330
  126.3 2.4 %collective-permute-start.18 = (f32[2,128]{1,0:T(2,128)S(1)}, f32[2,128]{1,0:T(2,128)S(1)}, u32[]{:S(2)}, u32[]{:S(2)}) collective-permute-start(f32[2,128]{1,0:T(2,128)S(1)} %get-tuple-element.81.part0_ref), channel_id=1, source_target_pairs={{0,192},{64,0},{128,64},{192,128},{1,193},{65,1},{129,65},{193,129... | collective-permute-start | bytes 3080 | tf_op jit(solution)/shard_map/ppermute | solution.py:330

commit v3 on v2

--- a/solution.py
+++ b/solution.py
@@ -15,7 +15,7 @@
 CHUNKS = TILE // LANES
 PRODUCT_ROWS = SLOTS * CHUNKS
 MESSAGE_ROWS = PRODUCT_ROWS + 8
-FINE = (0, 1, 2, 3)
+FINE = (0, 1)
 
 damping = 1.0
 

time: 130 us -> 126 us (0.969)
  blocking collectives: 63.6 us -> 61.6 us
  starting transfers between devices: 37.8 us -> 36.1 us
    all_to_all x4, blocking collectives: 63.6 us -> 61.6 us  [exchange(): own = lax.all_to_all(message, ('x', 'z'), 0, 0)]
where the time goes in v3:
time: 126 us; the launch traced here: 125 us
  blocking collectives  61.6 us (49%)
  starting transfers between devices  36.1 us (29%)
  waiting for transfers between devices  12.3 us (10%)
  Pallas kernels  8.53 us (7%)
  matrix products  3.01 us (2%)
  other arithmetic  1.95 us (2%)
    all_to_all x4, blocking collectives, exchange(): own = lax.all_to_all(message, ('x', 'z'), 0, 0)  61.6 us
    ppermute x15, starting transfers between devices, shifts_along_rows(): lax.ppermute(values, 'rows', [(i, (i + step) % n) for i in range(n)])  19.8 us
    ppermute x4, starting transfers between devices, exchange(): return (own, lax.ppermute(own, 'core', [(0, 1), (1, 0)]))  16.3 us
    pallas_call x11, Pallas kernels, call(): pl.pallas_call(kernel, out_shape=out_shape, in_specs=[pl.BlockSpec(memory...  8.53 us
    ppermute x15, waiting for transfers between devices, shifts_along_rows(): lax.ppermute(values, 'rows', [(i, (i + step) % n) for i in range(n)])  7.67 us
    ppermute x4, waiting for transfers between devices, exchange(): return (own, lax.ppermute(own, 'core', [(0, 1), (1, 0)]))  4.65 us
  transfers between devices with their start and end apart: 19, of which 12 were waited for; matrix products, arithmetic and copies ran while one was open for 1% of the time, Pallas kernels for 1%

profile of v3, /device:TPU:1, one launch (start us, length us, event | category | flops | bytes accessed | tf_op | source)
XLA Modules:
  0.0 125.2 jit_solution(1697583858124454029)
XLA Ops:
  0.7 1.2 multiply_convert_fusion
  2.0 0.8 fusion
  2.9 2.0 %fusion.7 = f32[4,1,512]{2,1,0:T(1,128)S(1)} fusion(bf16[4,512,1]{1,0,2:T(4,128)(2,1)S(1)} %fusion, bf16[1,4,512,512]{3,2,1,0:T(8,128)(2,1)} %param.8), kind=kOutput, calls=%fused_computation.21 | convolution fusion | flops 2097152 | bytes 2109440 | tf_op jit(solution)/shard_map/sab,sa->sb/dot_general | solution.py:362
  5.0 2.1 %collective-permute-start = (f32[2,512]{1,0:T(2,128)S(1)}, f32[2,512]{1,0:T(2,128)S(1)}, u32[]{:S(2)}, u32[]{:S(2)}) collective-permute-start(f32[2,512]{1,0:T(2,128)S(1)} %fusion.5.part0_ref), channel_id=1, source_target_pairs={{0,64},{64,128},{128,192},{192,0},{1,65},{65,129},{129,193},{193,1... | collective-permute-start | bytes 12296 | tf_op jit(solution)/shard_map/ppermute | solution.py:330
  7.2 2.6 %collective-permute-start.1 = (f32[2,512]{1,0:T(2,128)S(1)}, f32[2,512]{1,0:T(2,128)S(1)}, u32[]{:S(2)}, u32[]{:S(2)}) collective-permute-start(f32[2,512]{1,0:T(2,128)S(1)} %fusion.5.part0_ref), channel_id=1, source_target_pairs={{0,128},{64,192},{128,0},{192,64},{1,129},{65,193},{129,1},{193,65... | collective-permute-start | bytes 12296 | tf_op jit(solution)/shard_map/ppermute | solution.py:330
  9.8 1.1 collective-permute-start.2
  12.5 1.0 shard_map.97
  13.6 20.8 %all_to_all.20.own_ref = bf16[32,40,128]{2,1,0:T(8,128)(2,1)S(1)} all-to-all(bf16[32,40,128]{2,1,0:T(8,128)(2,1)S(1)} %get-tuple-element.50), channel_id=1, replica_groups=mesh['rows'=4,'x'=4,'z'=8,'core'=2] {'x','z'}, dimensions={0} | all-to-all | bytes 655360 | tf_op jit(solution)/shard_map/all_to_all | solution.py:336
  34.3 4.4 %collective-permute-start.3 = (bf16[32,40,128]{2,1,0:T(8,128)(2,1)S(1)}, bf16[32,40,128]{2,1,0:T(8,128)(2,1)S(1)}, u32[]{:S(2)}, u32[]{:S(2)}) collective-permute-start(bf16[32,40,128]{2,1,0:T(8,128)(2,1)S(1)} %all_to_all.20.own_ref), channel_id=1, source_target_pairs={{0,1},{1,0},{2,3},{3,2},{4,5},{5,4},{6,7},{7,6},{8,9},{9,8},{10,11... | collective-permute-start | bytes 983048 | tf_op jit(solution)/shard_map/ppermute | solution.py:337
  38.7 1.3 %collective-permute-done.3.other_ref = bf16[32,40,128]{2,1,0:T(8,128)(2,1)S(1)} collective-permute-done((bf16[32,40,128]{2,1,0:T(8,128)(2,1)S(1)}, bf16[32,40,128]{2,1,0:T(8,128)(2,1)S(1)}, u32[]{:S(2)}, u32[]{:S(2)}) %collective-permute-start.3) | collective-permute-done | bytes 327712 | tf_op jit(solution)/shard_map/ppermute | solution.py:337
  40.0 1.0 shard_map.98
  41.4 3.3 %collective-permute-start.5 = (f32[2,640]{1,0:T(2,128)S(1)}, f32[2,640]{1,0:T(2,128)S(1)}, u32[]{:S(2)}, u32[]{:S(2)}) collective-permute-start(f32[2,640]{1,0:T(2,128)S(1)} %get-tuple-element.53.refs_10_), channel_id=1, source_target_pairs={{0,128},{64,192},{128,0},{192,64},{1,129},{65,193},{129,1},{193,65... | collective-permute-start | bytes 15368 | tf_op jit(solution)/shard_map/ppermute | solution.py:330
  45.7 1.4 %collective-permute-done.6.refs_13_ = f32[2,640]{1,0:T(2,128)S(1)} collective-permute-done((f32[2,640]{1,0:T(2,128)S(1)}, f32[2,640]{1,0:T(2,128)S(1)}, u32[]{:S(2)}, u32[]{:S(2)}) %collective-permute-start.6) | collective-permute-done | bytes 5152 | tf_op jit(solution)/shard_map/ppermute | solution.py:330
  47.9 13.9 %all_to_all.21.own_ref = bf16[32,40,128]{2,1,0:T(8,128)(2,1)S(1)} all-to-all(bf16[32,40,128]{2,1,0:T(8,128)(2,1)S(1)} %get-tuple-element.57), channel_id=1, replica_groups=mesh['rows'=4,'x'=4,'z'=8,'core'=2] {'x','z'}, dimensions={0} | all-to-all | bytes 655360 | tf_op jit(solution)/shard_map/all_to_all | solution.py:336
  61.9 4.4 %collective-permute-start.7 = (bf16[32,40,128]{2,1,0:T(8,128)(2,1)S(1)}, bf16[32,40,128]{2,1,0:T(8,128)(2,1)S(1)}, u32[]{:S(2)}, u32[]{:S(2)}) collective-permute-start(bf16[32,40,128]{2,1,0:T(8,128)(2,1)S(1)} %all_to_all.21.own_ref), channel_id=1, source_target_pairs={{0,1},{1,0},{2,3},{3,2},{4,5},{5,4},{6,7},{7,6},{8,9},{9,8},{10,11... | collective-permute-start | bytes 983048 | tf_op jit(solution)/shard_map/ppermute | solution.py:337
  66.2 1.3 %collective-permute-done.7.other_ref = bf16[32,40,128]{2,1,0:T(8,128)(2,1)S(1)} collective-permute-done((bf16[32,40,128]{2,1,0:T(8,128)(2,1)S(1)}, bf16[32,40,128]{2,1,0:T(8,128)(2,1)S(1)}, u32[]{:S(2)}, u32[]{:S(2)}) %collective-permute-start.7) | collective-permute-done | bytes 327712 | tf_op jit(solution)/shard_map/ppermute | solution.py:337
  67.5 1.0 shard_map.100
  68.5 1.4 %collective-permute-start.10 = (f32[2,640]{1,0:T(2,128)S(1)}, f32[2,640]{1,0:T(2,128)S(1)}, u32[]{:S(2)}, u32[]{:S(2)}) collective-permute-start(f32[2,640]{1,0:T(2,128)S(1)} %get-tuple-element.63.refs_12_), channel_id=1, source_target_pairs={{0,192},{64,0},{128,64},{192,128},{1,193},{65,1},{129,65},{193,129... | collective-permute-start | bytes 15368 | tf_op jit(solution)/shard_map/ppermute | solution.py:330
  70.1 1.6 %collective-permute-start.9 = (f32[2,640]{1,0:T(2,128)S(1)}, f32[2,640]{1,0:T(2,128)S(1)}, u32[]{:S(2)}, u32[]{:S(2)}) collective-permute-start(f32[2,640]{1,0:T(2,128)S(1)} %get-tuple-element.63.refs_12_), channel_id=1, source_target_pairs={{0,128},{64,192},{128,0},{192,64},{1,129},{65,193},{129,1},{193,65... | collective-permute-start | bytes 15368 | tf_op jit(solution)/shard_map/ppermute | solution.py:330
  71.7 1.9 %collective-permute-done.8.refs_13_ = f32[2,640]{1,0:T(2,128)S(1)} collective-permute-done((f32[2,640]{1,0:T(2,128)S(1)}, f32[2,640]{1,0:T(2,128)S(1)}, u32[]{:S(2)}, u32[]{:S(2)}) %collective-permute-start.8) | collective-permute-done | bytes 5152 | tf_op jit(solution)/shard_map/ppermute | solution.py:330
  74.8 14.0 %all_to_all.22.own_ref = bf16[32,24,128]{2,1,0:T(8,128)(2,1)S(1)} all-to-all(bf16[32,24,128]{2,1,0:T(8,128)(2,1)S(1)} %get-tuple-element.66), channel_id=1, replica_groups=mesh['rows'=4,'x'=4,'z'=8,'core'=2] {'x','z'}, dimensions={0} | all-to-all | bytes 393216 | tf_op jit(solution)/shard_map/all_to_all | solution.py:336
  88.8 3.8 %collective-permute-start.11 = (bf16[32,24,128]{2,1,0:T(8,128)(2,1)S(1)}, bf16[32,24,128]{2,1,0:T(8,128)(2,1)S(1)}, u32[]{:S(2)}, u32[]{:S(2)}) collective-permute-start(bf16[32,24,128]{2,1,0:T(8,128)(2,1)S(1)} %all_to_all.22.own_ref), channel_id=1, source_target_pairs={{0,1},{1,0},{2,3},{3,2},{4,5},{5,4},{6,7},{7,6},{8,9},{9,8},{10,11... | collective-permute-start | bytes 589832 | tf_op jit(solution)/shard_map/ppermute | solution.py:337
  92.6 1.1 collective-permute-done.11.other_ref
  93.7 0.8 shard_map.102
  95.0 3.3 %collective-permute-start.13 = (f32[2,640]{1,0:T(2,128)S(1)}, f32[2,640]{1,0:T(2,128)S(1)}, u32[]{:S(2)}, u32[]{:S(2)}) collective-permute-start(f32[2,640]{1,0:T(2,128)S(1)} %get-tuple-element.72.refs_12_), channel_id=1, source_target_pairs={{0,128},{64,192},{128,0},{192,64},{1,129},{65,193},{129,1},{193,65... | collective-permute-start | bytes 15368 | tf_op jit(solution)/shard_map/ppermute | solution.py:330
  98.3 1.1 collective-permute-done.13.refs_14_
  99.4 1.4 %collective-permute-done.14.refs_15_ = f32[2,640]{1,0:T(2,128)S(1)} collective-permute-done((f32[2,640]{1,0:T(2,128)S(1)}, f32[2,640]{1,0:T(2,128)S(1)}, u32[]{:S(2)}, u32[]{:S(2)}) %collective-permute-start.14) | collective-permute-done | bytes 5152 | tf_op jit(solution)/shard_map/ppermute | solution.py:330
  101.5 12.9 %all_to_all.23.own_ref = bf16[32,24,128]{2,1,0:T(8,128)(2,1)S(1)} all-to-all(bf16[32,24,128]{2,1,0:T(8,128)(2,1)S(1)} %get-tuple-element.75), channel_id=1, replica_groups=mesh['rows'=4,'x'=4,'z'=8,'core'=2] {'x','z'}, dimensions={0} | all-to-all | bytes 393216 | tf_op jit(solution)/shard_map/all_to_all | solution.py:336
  114.4 3.8 %collective-permute-start.15 = (bf16[32,24,128]{2,1,0:T(8,128)(2,1)S(1)}, bf16[32,24,128]{2,1,0:T(8,128)(2,1)S(1)}, u32[]{:S(2)}, u32[]{:S(2)}) collective-permute-start(bf16[32,24,128]{2,1,0:T(8,128)(2,1)S(1)} %all_to_all.23.own_ref), channel_id=1, source_target_pairs={{0,1},{1,0},{2,3},{3,2},{4,5},{5,4},{6,7},{7,6},{8,9},{9,8},{10,11... | collective-permute-start | bytes 589832 | tf_op jit(solution)/shard_map/ppermute | solution.py:337
  118.2 1.1 collective-permute-done.15.other_ref
  119.6 2.1 %collective-permute-start.17 = (f32[2,128]{1,0:T(2,128)S(1)}, f32[2,128]{1,0:T(2,128)S(1)}, u32[]{:S(2)}, u32[]{:S(2)}) collective-permute-start(f32[2,128]{1,0:T(2,128)S(1)} %get-tuple-element.81.part0_ref), channel_id=1, source_target_pairs={{0,128},{64,192},{128,0},{192,64},{1,129},{65,193},{129,1},{193,65... | collective-permute-start | bytes 3080 | tf_op jit(solution)/shard_map/ppermute | solution.py:330
  121.7 1.2 collective-permute-start.18
  (48 shorter events, 9.3 us)
Async XLA Ops:
  0.6 11.0 %copy-start.1 = (f32[65536]{0:T(1024)S(1)}, f32[65536]{0:T(1024)}, u32[]{:S(2)}) copy-start(f32[65536]{0:T(1024)} %param.13) | copy-start | bytes 786436
  0.6 10.9 %copy-start.6 = (s32[1,4]{1,0:T(1,128)S(1)}, s32[1,4]{1,0:T(1,128)}, u32[]{:S(2)}) copy-start(s32[1,4]{1,0:T(1,128)} %param.9) | copy-start | bytes 52
  0.7 11.9 %copy-start = (bf16[1,4,512,512]{3,2,1,0:T(8,128)(2,1)S(1)}, bf16[1,4,512,512]{3,2,1,0:T(8,128)(2,1)}, u32[]{:S(2)}) copy-start(bf16[1,4,512,512]{3,2,1,0:T(8,128)(2,1)} %param.8) | copy-start | bytes 6291460
  0.7 4.2 %copy-start.5 = (s32[1,4]{1,0:T(1,128)S(1)}, s32[1,4]{1,0:T(1,128)}, u32[]{:S(2)}) copy-start(s32[1,4]{1,0:T(1,128)} %param.10) | copy-start | bytes 52
  0.7 4.1 %copy-start.4 = (s32[1,4]{1,0:T(1,128)S(1)}, s32[1,4]{1,0:T(1,128)}, u32[]{:S(2)}) copy-start(s32[1,4]{1,0:T(1,128)} %param.11) | copy-start | bytes 52
  0.7 10.9 %copy-start.2 = (f32[1024]{0:T(1024)S(1)}, f32[1024]{0:T(1024)}, u32[]{:S(2)}) copy-start(f32[1024]{0:T(1024)} %param.14) | copy-start | bytes 12292
  0.7 10.9 %copy-start.3 = (f32[1024]{0:T(1024)S(1)}, f32[1024]{0:T(1024)}, u32[]{:S(2)}) copy-start(f32[1024]{0:T(1024)} %param.15) | copy-start | bytes 12292
  5.0 7.2 %collective-permute-start = (f32[2,512]{1,0:T(2,128)S(1)}, f32[2,512]{1,0:T(2,128)S(1)}, u32[]{:S(2)}, u32[]{:S(2)}) collective-permute-start(f32[2,512]{1,0:T(2,128)S(1)} %fusion.5.part0_ref), channel_id=1, source_target_pairs={{0,64},{64,128},{128,192},{192,0},{1,65},{65,129},{129,193},{193,1... | collective-permute-start | bytes 12296 | tf_op jit(solution)/shard_map/ppermute | solution.py:330
  7.2 5.1 %collective-permute-start.1 = (f32[2,512]{1,0:T(2,128)S(1)}, f32[2,512]{1,0:T(2,128)S(1)}, u32[]{:S(2)}, u32[]{:S(2)}) collective-permute-start(f32[2,512]{1,0:T(2,128)S(1)} %fusion.5.part0_ref), channel_id=1, source_target_pairs={{0,128},{64,192},{128,0},{192,64},{1,129},{65,193},{129,1},{193,65... | collective-permute-start | bytes 12296 | tf_op jit(solution)/shard_map/ppermute | solution.py:330
  9.8 2.8 %collective-permute-start.2 = (f32[2,512]{1,0:T(2,128)S(1)}, f32[2,512]{1,0:T(2,128)S(1)}, u32[]{:S(2)}, u32[]{:S(2)}) collective-permute-start(f32[2,512]{1,0:T(2,128)S(1)} %fusion.5.part0_ref), channel_id=1, source_target_pairs={{0,192},{64,0},{128,64},{192,128},{1,193},{65,1},{129,65},{193,129... | collective-permute-start | bytes 12296 | tf_op jit(solution)/shard_map/ppermute | solution.py:330
  34.3 5.6 %collective-permute-start.3 = (bf16[32,40,128]{2,1,0:T(8,128)(2,1)S(1)}, bf16[32,40,128]{2,1,0:T(8,128)(2,1)S(1)}, u32[]{:S(2)}, u32[]{:S(2)}) collective-permute-start(bf16[32,40,128]{2,1,0:T(8,128)(2,1)S(1)} %all_to_all.20.own_ref), channel_id=1, source_target_pairs={{0,1},{1,0},{2,3},{3,2},{4,5},{5,4},{6,7},{7,6},{8,9},{9,8},{10,11... | collective-permute-start | bytes 983048 | tf_op jit(solution)/shard_map/ppermute | solution.py:337
  41.0 4.4 %collective-permute-start.4 = (f32[2,640]{1,0:T(2,128)S(1)}, f32[2,640]{1,0:T(2,128)S(1)}, u32[]{:S(2)}, u32[]{:S(2)}) collective-permute-start(f32[2,640]{1,0:T(2,128)S(1)} %get-tuple-element.53.refs_10_), channel_id=1, source_target_pairs={{0,64},{64,128},{128,192},{192,0},{1,65},{65,129},{129,193},{193,1... | collective-permute-start | bytes 15368 | tf_op jit(solution)/shard_map/ppermute | solution.py:330
  41.4 4.4 %collective-permute-start.5 = (f32[2,640]{1,0:T(2,128)S(1)}, f32[2,640]{1,0:T(2,128)S(1)}, u32[]{:S(2)}, u32[]{:S(2)}) collective-permute-start(f32[2,640]{1,0:T(2,128)S(1)} %get-tuple-element.53.refs_10_), channel_id=1, source_target_pairs={{0,128},{64,192},{128,0},{192,64},{1,129},{65,193},{129,1},{193,65... | collective-permute-start | bytes 15368 | tf_op jit(solution)/shard_map/ppermute | solution.py:330
  44.7 2.5 %collective-permute-start.6 = (f32[2,640]{1,0:T(2,128)S(1)}, f32[2,640]{1,0:T(2,128)S(1)}, u32[]{:S(2)}, u32[]{:S(2)}) collective-permute-start(f32[2,640]{1,0:T(2,128)S(1)} %get-tuple-element.53.refs_10_), channel_id=1, source_target_pairs={{0,192},{64,0},{128,64},{192,128},{1,193},{65,1},{129,65},{193,129... | collective-permute-start | bytes 15368 | tf_op jit(solution)/shard_map/ppermute | solution.py:330
  61.9 5.6 %collective-permute-start.7 = (bf16[32,40,128]{2,1,0:T(8,128)(2,1)S(1)}, bf16[32,40,128]{2,1,0:T(8,128)(2,1)S(1)}, u32[]{:S(2)}, u32[]{:S(2)}) collective-permute-start(bf16[32,40,128]{2,1,0:T(8,128)(2,1)S(1)} %all_to_all.21.own_ref), channel_id=1, source_target_pairs={{0,1},{1,0},{2,3},{3,2},{4,5},{5,4},{6,7},{7,6},{8,9},{9,8},{10,11... | collective-permute-start | bytes 983048 | tf_op jit(solution)/shard_map/ppermute | solution.py:337
  68.5 3.2 %collective-permute-start.10 = (f32[2,640]{1,0:T(2,128)S(1)}, f32[2,640]{1,0:T(2,128)S(1)}, u32[]{:S(2)}, u32[]{:S(2)}) collective-permute-start(f32[2,640]{1,0:T(2,128)S(1)} %get-tuple-element.63.refs_12_), channel_id=1, source_target_pairs={{0,192},{64,0},{128,64},{192,128},{1,193},{65,1},{129,65},{193,129... | collective-permute-start | bytes 15368 | tf_op jit(solution)/shard_map/ppermute | solution.py:330
  70.0 3.7 %collective-permute-start.8 = (f32[2,640]{1,0:T(2,128)S(1)}, f32[2,640]{1,0:T(2,128)S(1)}, u32[]{:S(2)}, u32[]{:S(2)}) collective-permute-start(f32[2,640]{1,0:T(2,128)S(1)} %get-tuple-element.63.refs_12_), channel_id=1, source_target_pairs={{0,64},{64,128},{128,192},{192,0},{1,65},{65,129},{129,193},{193,1... | collective-permute-start | bytes 15368 | tf_op jit(solution)/shard_map/ppermute | solution.py:330
  70.1 4.0 %collective-permute-start.9 = (f32[2,640]{1,0:T(2,128)S(1)}, f32[2,640]{1,0:T(2,128)S(1)}, u32[]{:S(2)}, u32[]{:S(2)}) collective-permute-start(f32[2,640]{1,0:T(2,128)S(1)} %get-tuple-element.63.refs_12_), channel_id=1, source_target_pairs={{0,128},{64,192},{128,0},{192,64},{1,129},{65,193},{129,1},{193,65... | collective-permute-start | bytes 15368 | tf_op jit(solution)/shard_map/ppermute | solution.py:330
  88.8 4.8 %collective-permute-start.11 = (bf16[32,24,128]{2,1,0:T(8,128)(2,1)S(1)}, bf16[32,24,128]{2,1,0:T(8,128)(2,1)S(1)}, u32[]{:S(2)}, u32[]{:S(2)}) collective-permute-start(bf16[32,24,128]{2,1,0:T(8,128)(2,1)S(1)} %all_to_all.22.own_ref), channel_id=1, source_target_pairs={{0,1},{1,0},{2,3},{3,2},{4,5},{5,4},{6,7},{7,6},{8,9},{9,8},{10,11... | collective-permute-start | bytes 589832 | tf_op jit(solution)/shard_map/ppermute | solution.py:337
  94.5 3.8 %collective-permute-start.12 = (f32[2,640]{1,0:T(2,128)S(1)}, f32[2,640]{1,0:T(2,128)S(1)}, u32[]{:S(2)}, u32[]{:S(2)}) collective-permute-start(f32[2,640]{1,0:T(2,128)S(1)} %get-tuple-element.72.refs_12_), channel_id=1, source_target_pairs={{0,64},{64,128},{128,192},{192,0},{1,65},{65,129},{129,193},{193,1... | collective-permute-start | bytes 15368 | tf_op jit(solution)/shard_map/ppermute | solution.py:330
  95.0 4.4 %collective-permute-start.13 = (f32[2,640]{1,0:T(2,128)S(1)}, f32[2,640]{1,0:T(2,128)S(1)}, u32[]{:S(2)}, u32[]{:S(2)}) collective-permute-start(f32[2,640]{1,0:T(2,128)S(1)} %get-tuple-element.72.refs_12_), channel_id=1, source_target_pairs={{0,128},{64,192},{128,0},{192,64},{1,129},{65,193},{129,1},{193,65... | collective-permute-start | bytes 15368 | tf_op jit(solution)/shard_map/ppermute | solution.py:330
  98.3 2.5 %collective-permute-start.14 = (f32[2,640]{1,0:T(2,128)S(1)}, f32[2,640]{1,0:T(2,128)S(1)}, u32[]{:S(2)}, u32[]{:S(2)}) collective-permute-start(f32[2,640]{1,0:T(2,128)S(1)} %get-tuple-element.72.refs_12_), channel_id=1, source_target_pairs={{0,192},{64,0},{128,64},{192,128},{1,193},{65,1},{129,65},{193,129... | collective-permute-start | bytes 15368 | tf_op jit(solution)/shard_map/ppermute | solution.py:330
  114.4 4.8 %collective-permute-start.15 = (bf16[32,24,128]{2,1,0:T(8,128)(2,1)S(1)}, bf16[32,24,128]{2,1,0:T(8,128)(2,1)S(1)}, u32[]{:S(2)}, u32[]{:S(2)}) collective-permute-start(bf16[32,24,128]{2,1,0:T(8,128)(2,1)S(1)} %all_to_all.23.own_ref), channel_id=1, source_target_pairs={{0,1},{1,0},{2,3},{3,2},{4,5},{5,4},{6,7},{7,6},{8,9},{9,8},{10,11... | collective-permute-start | bytes 589832 | tf_op jit(solution)/shard_map/ppermute | solution.py:337
  119.5 4.1 %collective-permute-start.16 = (f32[2,128]{1,0:T(2,128)S(1)}, f32[2,128]{1,0:T(2,128)S(1)}, u32[]{:S(2)}, u32[]{:S(2)}) collective-permute-start(f32[2,128]{1,0:T(2,128)S(1)} %get-tuple-element.81.part0_ref), channel_id=1, source_target_pairs={{0,64},{64,128},{128,192},{192,0},{1,65},{65,129},{129,193},{193,1... | collective-permute-start | bytes 3080 | tf_op jit(solution)/shard_map/ppermute | solution.py:330
  119.6 4.0 %collective-permute-start.17 = (f32[2,128]{1,0:T(2,128)S(1)}, f32[2,128]{1,0:T(2,128)S(1)}, u32[]{:S(2)}, u32[]{:S(2)}) collective-permute-start(f32[2,128]{1,0:T(2,128)S(1)} %get-tuple-element.81.part0_ref), channel_id=1, source_target_pairs={{0,128},{64,192},{128,0},{192,64},{1,129},{65,193},{129,1},{193,65... | collective-permute-start | bytes 3080 | tf_op jit(solution)/shard_map/ppermute | solution.py:330
  121.7 2.7 %collective-permute-start.18 = (f32[2,128]{1,0:T(2,128)S(1)}, f32[2,128]{1,0:T(2,128)S(1)}, u32[]{:S(2)}, u32[]{:S(2)}) collective-permute-start(f32[2,128]{1,0:T(2,128)S(1)} %get-tuple-element.81.part0_ref), channel_id=1, source_target_pairs={{0,192},{64,0},{128,64},{192,128},{1,193},{65,1},{129,65},{193,129... | collective-permute-start | bytes 3080 | tf_op jit(solution)/shard_map/ppermute | solution.py:330
